TPU v7x, 128 devices: a whole 4x4x4 slice. The times are simulated.
128 devices in a mesh: row: 16 (over x, y_hi, core), col: 8 (over y_lo, z).
Axes of the slice: x: 4, y: 4 (y_hi: 2, y_lo: 2; y = y_hi * 2 + y_lo), z: 4, core: 2. Of those that a mesh axis runs over, the one named last changes fastest.
Arguments:
- vectors_in: float32 [1024, 196608], P(('row', 'col')), may hold values from -6 to 6
- panel_first: float32 [196608, 256], P('row', 'col'), may hold values from -0.15625 to 0.15625
- panel_second: float32 [196608, 256], P('row', 'col'), may hold values from -0.15625 to 0.15625
- factor_first: float32 [256, 256], replicated, may hold values from -0.375 to 0.375
- factor_second: float32 [256, 256], replicated, may hold values from -0.375 to 0.375
Outputs:
- vectors_out: float32 [1024, 196608], P('col', 'row')
All inputs are finite; a program needn't handle non-finite values.
Results may differ from a plain program's by a relative error of at most 0.00007.
Values sent between devices are 32-bit elements; how exact they have to be, the bound alone decides.
No kernel may reach another device: no remote copies, remote signals or barrier semaphores. Data moves between devices by JAX's collectives and lax.ppermute only.
A program may use at most 192 MiB of HBM per device.

v0:
```python
import jax
import jax.numpy as jnp
from jax import lax
from jax.sharding import PartitionSpec as P


def matmul(left, right):
    return jnp.dot(left, right, precision=lax.Precision.HIGHEST, preferred_element_type=jnp.float32)


def times_transposed(left, right):
    return lax.dot_general(
        left,
        right,
        (((1,), (1,)), ((), ())),
        precision=lax.Precision.HIGHEST,
        preferred_element_type=jnp.float32,
    )


def apply_panels(zt, v_first, v_second, f_first, f_second, single_sum):
    for panel, factor in ((v_first, f_first), (v_second, f_second)):
        weights = single_sum(matmul(zt, panel))
        zt = zt - times_transposed(matmul(weights, factor.T), panel)
    return zt


def body(vectors_in, panel_first, panel_second, factor_first, factor_second):
    row_count = lax.axis_size("row")
    col_count = lax.axis_size("col")
    moved = lax.all_to_all(
        lax.all_to_all(vectors_in, "row", split_axis=1, concat_axis=0, tiled=True),
        "col",
        split_axis=0,
        concat_axis=0,
        tiled=True,
    )
    per_device = vectors_in.shape[0]
    group = row_count // col_count
    local_rows = moved.shape[1]
    zt = (
        moved.reshape(col_count, group, per_device, local_rows)
        .transpose(1, 0, 2, 3)
        .reshape(-1, local_rows)
    )
    v_first, v_second = (
        lax.all_gather(panel_first, "col", axis=1, tiled=True),
        lax.all_gather(panel_second, "col", axis=1, tiled=True),
    )

    def single_sum(term):
        return lax.psum(term, "row")

    output = apply_panels(zt, v_first, v_second, factor_first, factor_second, single_sum)
    return output


def solution(mesh):
    return jax.shard_map(
        body,
        mesh=mesh,
        in_specs=(P(("row", "col"), None), P("row", "col"), P("row", "col"), P(), P()),
        out_specs=P("col", "row"),
        check_vma=False,
    )
```

profile of v0, /device:TPU:0, one launch (start us, length us, event | category | flops | bytes accessed | tf_op | source)
XLA Modules:
  0.0 732.1 jit_solution(889351538591369243)
XLA Ops:
  6.5 0.0 copy-start
  6.5 0.0 all-gather.3.cloned.1.call-start
  6.5 0.7 all-gather.3.cloned.1.call-update
  7.3 0.0 all-reduce.3.cloned.1.call-start
  7.3 92.6 %all_to_all.25 = f32[8,16,12288]{2,0,1:T(8,128)S(1)} all-to-all(f32[8,16,12288]{2,0,1:T(8,128)} %bitcast.24), channel_id=1, replica_groups=mesh['row'=16,'col'=8] {'row'}, dimensions={1} | all-to-all | bytes 12582912 | tf_op jit(solution)/shard_map/all_to_all | solution.py:32
  99.9 148.2 %all_to_all.26 = f32[8,16,12288]{2,1,0:T(8,128)S(1)} all-to-all(f32[8,16,12288]{2,1,0:T(8,128)S(1)} %bitcast.23), channel_id=1, replica_groups=mesh['row'=16,'col'=8] {'col'}, dimensions={0} | all-to-all | bytes 12582912 | tf_op jit(solution)/shard_map/all_to_all | solution.py:31
  248.1 3.2 copy.6
  251.3 25.5 %all-gather.3.cloned.1.call-done = f32[12288,256]{0,1:T(8,128)} async-done(((f32[12288,32]{0,1:T(8,128)}), f32[12288,256]{0,1:T(8,128)}) %all-gather.3.cloned.1.call-update) | async-done | bytes 12582928 | tf_op jit(solution)/shard_map/all_gather | solution.py:47
  276.7 16.1 %fusion = f32[128,256]{1,0:T(8,128)} fusion(f32[128,12288]{1,0:T(8,128)} %bitcast.20, f32[12288,256]{0,1:T(8,128)} %all-gather.3.cloned.1.call-done), kind=kOutput, calls=%fused_computation.2 | convolution fusion | flops 4831838208 | bytes 19005440 | tf_op jit(solution)/shard_map/dot_general | solution.py:8
  292.9 0.0 all-reduce.3.cloned.1.call-update
  292.9 0.0 all-gather.5.cloned.1.call-start
  292.9 0.7 all-gather.5.cloned.1.call-update
  293.6 0.2 all-reduce.5.cloned.1.call-start
  293.9 132.4 %all-reduce.3.cloned.1.call-done = f32[128,256]{1,0:T(8,128)} async-done(((f32[128,256]{1,0:T(8,128)}), f32[128,256]{1,0:T(8,128)}) %all-reduce.3.cloned.1.call-update) | async-done | bytes 131088 | tf_op jit(solution)/shard_map/psum | solution.py:52
  426.3 0.0 copy-done
  426.3 1.3 fusion.1
  427.6 12.4 %convolution_subtract_fusion.1 = f32[128,12288]{1,0:T(8,128)} fusion(f32[128,12288]{1,0:T(8,128)} %bitcast.21, f32[128,256]{1,0:T(8,128)S(1)} %fusion.1, f32[12288,256]{0,1:T(8,128)} %all-gather.3.cloned.1.call-done), kind=kOutput, calls=%fused_computation.1 | convolution fusion | flops 4833411072 | bytes 25296896 | tf_op jit(solution)/shard_map/dot_general | solution.py:12
  440.0 120.7 %all-gather.5.cloned.1.call-done = f32[12288,256]{0,1:T(8,128)} async-done(((f32[12288,32]{0,1:T(8,128)}), f32[12288,256]{0,1:T(8,128)}) %all-gather.5.cloned.1.call-update) | async-done | bytes 12582928 | tf_op jit(solution)/shard_map/all_gather | solution.py:48
  560.7 16.1 %fusion.2 = f32[128,256]{1,0:T(8,128)} fusion(f32[128,12288]{1,0:T(8,128)} %convolution_subtract_fusion.1, f32[12288,256]{0,1:T(8,128)} %all-gather.5.cloned.1.call-done), kind=kOutput, calls=%fused_computation.4 | convolution fusion | flops 4831838208 | bytes 19005440 | tf_op jit(solution)/shard_map/dot_general | solution.py:8
  576.8 0.0 all-reduce.5.cloned.1.call-update
  576.8 135.0 %all-reduce.5.cloned.1.call-done = f32[128,256]{1,0:T(8,128)} async-done(((f32[128,256]{1,0:T(8,128)}), f32[128,256]{1,0:T(8,128)}) %all-reduce.5.cloned.1.call-update) | async-done | bytes 131088 | tf_op jit(solution)/shard_map/psum | solution.py:52
  711.8 1.3 fusion.3
  713.1 0.0 copy-start.1
  713.1 12.5 %convolution_subtract_fusion = f32[128,12288]{1,0:T(8,128)} fusion(f32[128,12288]{1,0:T(8,128)} %convolution_subtract_fusion.1, f32[128,256]{1,0:T(8,128)S(1)} %fusion.3, f32[12288,256]{0,1:T(8,128)} %all-gather.5.cloned.1.call-done), kind=kOutput, calls=%fused_computation | convolution fusion | flops 4833411072 | bytes 25296896 | tf_op jit(solution)/shard_map/dot_general | solution.py:12
  (3 shorter events, 0.0 us)
Async XLA Ops:
  6.5 419.7 %copy-start = (f32[256,256]{1,0:T(8,128)S(1)}, f32[256,256]{1,0:T(8,128)}, u32[]{:S(2)}) copy-start(f32[256,256]{1,0:T(8,128)} %param.8) | copy-start | bytes 786436
  6.5 270.2 %all-gather.3.cloned.1.call-start = ((), (), s32[]{:S(2)}) async-start(), calls=%async_computation.2 | async-start | bytes 14155776 | tf_op jit(solution)/shard_map/all_gather | solution.py:47
  7.3 419.0 %all-reduce.3.cloned.1.call-start = ((), (), s32[]{:S(2)}) async-start(), calls=%async_computation.3 | async-start | bytes 262144 | tf_op jit(solution)/shard_map/psum | solution.py:52
  292.9 267.8 %all-gather.5.cloned.1.call-start = ((), (), s32[]{:S(2)}) async-start(), calls=%async_computation.4 | async-start | bytes 14155776 | tf_op jit(solution)/shard_map/all_gather | solution.py:48
  293.6 418.2 %all-reduce.5.cloned.1.call-start = ((), (), s32[]{:S(2)}) async-start(), calls=%async_computation.5 | async-start | bytes 262144 | tf_op jit(solution)/shard_map/psum | solution.py:52
  440.0 271.8 %copy-start.2 = (f32[256,256]{1,0:T(8,128)S(1)}, f32[256,256]{1,0:T(8,128)}, u32[]{:S(2)}) copy-start(f32[256,256]{1,0:T(8,128)} %param.9) | copy-start | bytes 786436
  713.1 12.5 %copy-start.1 = (f32[256,256]{1,0:T(8,128)S(1)}, f32[256,256]{1,0:T(8,128)}, u32[]{:S(2)}) copy-start(f32[256,256]{1,0:T(8,128)} %param.8) | copy-start | bytes 786436
Sparse Core Ops, SparseCore 0:
  9.0 267.6 all-gather.2
  293.0 133.2 all-reduce.2
  428.0 132.6 all-gather.4
  577.0 134.8 all-reduce.4
where the time goes:
time: 733 us; the launch traced here: 732 us
  waiting for transfers between devices  415 us (57%)
  blocking collectives  241 us (33%)
  matrix products  59.8 us (8%)
  between operations  13.2 us (2%)
    psum x2, waiting for transfers between devices, single_sum(): return lax.psum(term, 'row')  267 us
    all_to_all x1, blocking collectives, body(): lax.all_to_all(lax.all_to_all(vectors_in, 'row', split_axis=1, concat_axi...  148 us
    all_gather x1, waiting for transfers between devices, body(): lax.all_gather(panel_second, 'col', axis=1, tiled=True)  121 us
    all_to_all x1, blocking collectives, body(): lax.all_to_all(vectors_in, 'row', split_axis=1, concat_axis=0, tiled=True)  92.6 us
    dot_general x4, matrix products, matmul(): jnp.dot(left, right, precision=lax.Precision.HIGHEST, preferred_element_t...  34.9 us
    all_gather x1, waiting for transfers between devices, body(): lax.all_gather(panel_first, 'col', axis=1, tiled=True)  25.5 us
    dot_general x2, matrix products, times_transposed(): lax.dot_general(left, right, (((1,), (1,)), ((), ())), precision=lax.Prec...  24.9 us
  transfers between devices with their start and end apart: 4, of which 4 were waited for; matrix products, arithmetic and copies ran while one was open for 2% of the time, Pallas kernels for 0%

commit v1 on v0

v1 whole, which is shorter than its diff:
```python
import jax
import jax.numpy as jnp
from jax import lax
from jax.sharding import Mesh, PartitionSpec as P

CHIPS = ("block", "col")
CORES = 2


def dot(left, right, left_dim, right_dim, precision):
    return lax.dot_general(
        left,
        right,
        (((left_dim,), (right_dim,)), ((), ())),
        precision=precision,
        preferred_element_type=jnp.float32,
    )


def body(vectors_in, panel_first, panel_second, factor_first, factor_second):
    blocks, cols = lax.axis_size("block"), lax.axis_size("col")
    chips = blocks * cols
    held = vectors_in.shape[0]
    width = panel_first.shape[1] * cols
    part = panel_first.shape[0] // cols
    core = lax.axis_index("core")

    panels = jnp.concatenate([panel_first.T, panel_second.T], axis=0)
    panels = panels.reshape(-1, cols, part).transpose(1, 0, 2)
    own = lax.all_to_all(panels, "col", split_axis=0, concat_axis=0, tiled=True)
    other = lax.ppermute(own, "core", [(0, 1), (1, 0)])
    zero = core == 0
    panels = jnp.stack([jnp.where(zero, own, other), jnp.where(zero, other, own)], axis=2)
    panels = panels.reshape(cols, 2, width // cols, CORES * part)
    panels = panels.transpose(1, 0, 2, 3).reshape(2 * width, CORES * part)
    overlap = dot(panels[:width], panels[width:], 1, 1, lax.Precision.HIGHEST)

    zt = vectors_in.reshape(held, blocks, CORES, cols, part).transpose(1, 3, 0, 2, 4)
    zt = zt.reshape(chips, held, CORES * part)
    zt = lax.all_to_all(zt, CHIPS, split_axis=0, concat_axis=0, tiled=True)
    zt = zt.reshape(chips * held, CORES * part)

    partial = dot(zt, panels, 1, 1, lax.Precision.HIGH).reshape(chips, held, 2 * width)
    partial = jnp.concatenate([partial, overlap.reshape(chips, held, -1)], axis=2)
    pieces = lax.all_to_all(partial, CHIPS, split_axis=0, concat_axis=0, tiled=True)
    total = jnp.sum(pieces, axis=0)
    copies = jnp.broadcast_to(total[None], (chips,) + total.shape)
    total = lax.all_to_all(copies, CHIPS, split_axis=0, concat_axis=0, tiled=True)
    overlap = total[:, :, 2 * width :].reshape(width, width)
    total = total.reshape(chips * held, -1)
    first = dot(total[:, :width], factor_first, 1, 1, lax.Precision.HIGHEST)
    second = total[:, width : 2 * width] - dot(first, overlap, 1, 0, lax.Precision.HIGHEST)
    second = dot(second, factor_second, 1, 1, lax.Precision.HIGHEST)
    weights = jnp.concatenate([first, second], axis=1)

    zt = zt - dot(weights, panels, 1, 0, lax.Precision.HIGH)
    zt = zt.reshape(blocks, cols * held, CORES, part).transpose(2, 0, 1, 3)
    zt = zt.reshape(CORES * cols, cols * held, part)
    zt = lax.all_to_all(zt, ("core", "col"), split_axis=0, concat_axis=0, tiled=True)
    zt = zt.reshape(CORES, cols, cols * held, part).transpose(0, 2, 1, 3)
    return zt.reshape(CORES * cols * held, cols * part)


def solution(mesh):
    rows, cols = mesh.devices.shape
    split = Mesh(mesh.devices.reshape(rows // CORES, CORES, cols), ("block", "core", "col"))
    return jax.shard_map(
        body,
        mesh=split,
        in_specs=(
            P(("block", "core", "col"), None),
            P(("block", "core"), "col"),
            P(("block", "core"), "col"),
            P(),
            P(),
        ),
        out_specs=P("col", ("block", "core")),
        check_vma=False,
    )
```

time: 733 us -> 327 us (0.45)
  waiting for transfers between devices: 415 us -> 69.1 us
  blocking collectives: 241 us -> 136 us
  local copies, waits for them, and re-layouts: 3.17 us -> 57.5 us
  matrix products: 59.8 us -> 25.6 us
  other arithmetic: 0 us -> 17.8 us
  starting transfers between devices: 0.3 us -> 16.2 us
  between operations: 13.2 us -> 0.41 us
    psum x2 -> x0, waiting for transfers between devices: 267 us -> none  [single_sum(): return lax.psum(term, 'row')]
    all_gather x2 -> x0, waiting for transfers between devices: 146 us -> none  [the longest x1 121 us: body(): lax.all_gather(panel_second, 'col', axis=1, tiled=True)]
    all_to_all x2 -> x3, blocking collectives: 241 us -> 136 us  [the longest x1 75.4 us: body(): lax.all_to_all(zt, ('core', 'col'), split_axis=0, concat_axis=0, tiled=True)]
    all_to_all x0 -> x2, waiting for transfers between devices: none -> 63.4 us  [the longest x1 32.2 us: body(): zt = lax.all_to_all(zt, CHIPS, split_axis=0, concat_axis=0, tiled=True)]
    dot_general x6, matrix products: 59.8 us -> 25.6 us  [dot(): lax.dot_general(left, right, (((left_dim,), (right_dim,)), ((), ())), pre...]
    reshape x0 -> x6, local copies, waits for them, and re-layouts: none -> 24.3 us  [the longest x2 13.1 us: body(): zt = zt.reshape(blocks, cols * held, CORES, part).transpose(2, 0, 1, 3)]
    all_to_all x0 -> x2, starting transfers between devices: none -> 15.6 us  [the longest x1 9.22 us: body(): zt = lax.all_to_all(zt, CHIPS, split_axis=0, concat_axis=0, tiled=True)]
    another operation x0 -> x2, other arithmetic: none -> 15.5 us  [body(): jnp.stack([jnp.where(zero, own, other), jnp.where(zero, other, own)], axi...]
  transfers between devices with their start and end apart: 4 -> 3, of which waited for: 4 -> 3; matrix products, arithmetic and copies ran while one was open for 2% -> 15% of each run, Pallas kernels for 0% -> 0%
where the time goes in v1:
time: 327 us; the launch traced here: 323 us
  blocking collectives  136 us (42%)
  waiting for transfers between devices  69.1 us (21%)
  local copies, waits for them, and re-layouts  57.5 us (18%)
  matrix products  25.6 us (8%)
  other arithmetic  17.8 us (5%)
  starting transfers between devices  16.2 us (5%)
    all_to_all x1, blocking collectives, body(): lax.all_to_all(zt, ('core', 'col'), split_axis=0, concat_axis=0, tiled=True)  75.4 us
    all_to_all x1, blocking collectives, body(): lax.all_to_all(partial, CHIPS, split_axis=0, concat_axis=0, tiled=True)  35.5 us
    all_to_all x1, waiting for transfers between devices, body(): zt = lax.all_to_all(zt, CHIPS, split_axis=0, concat_axis=0, tiled=True)  32.2 us
    all_to_all x1, waiting for transfers between devices, body(): own = lax.all_to_all(panels, 'col', split_axis=0, concat_axis=0, tiled=True)  31.1 us
    dot_general x6, matrix products, dot(): lax.dot_general(left, right, (((left_dim,), (right_dim,)), ((), ())), pre...  25.6 us
    all_to_all x1, blocking collectives, body(): lax.all_to_all(copies, CHIPS, split_axis=0, concat_axis=0, tiled=True)  25.1 us
    another operation x2, other arithmetic, body(): jnp.stack([jnp.where(zero, own, other), jnp.where(zero, other, own)], axi...  15.5 us
    reshape x2, local copies, waits for them, and re-layouts, body(): zt = zt.reshape(blocks, cols * held, CORES, part).transpose(2, 0, 1, 3)  13.1 us
  transfers between devices with their start and end apart: 3, of which 3 were waited for; matrix products, arithmetic and copies ran while one was open for 15% of the time, Pallas kernels for 0%

profile of v1, /device:TPU:0, one launch (start us, length us, event | category | flops | bytes accessed | tf_op | source)
XLA Modules:
  0.0 322.7 jit_solution(14247615467802406428)
XLA Ops:
  0.0 2.1 pad_maximum_fusion.1
  2.2 1.9 copy.21
  4.1 6.4 %all-to-all-start.1 = ((f32[8,64,1536]{2,1,0:T(8,128)}), f32[8,64,1536]{2,1,0:T(8,128)S(1)}, u32[]{:S(2)}, u32[]{:S(2)}) async-start(f32[8,64,1536]{2,1,0:T(8,128)} %bitcast.47), calls=%async_computation.1 | async-start | bytes 6291456 | tf_op jit(solution)/shard_map/all_to_all | solution.py:30
  10.5 6.1 %copy.12 = f32[8,8,8,2,1536]{4,2,3,1,0:T(8,128)} copy(f32[8,8,8,2,1536]{4,2,1,3,0:T(8,128)} %bitcast.61) | data formatting | bytes 12582912 | tf_op jit(solution)/shard_map/transpose | solution.py:38
  16.6 31.1 %all-to-all-done.1 = f32[8,64,1536]{2,1,0:T(8,128)S(1)} async-done(((f32[8,64,1536]{2,1,0:T(8,128)}), f32[8,64,1536]{2,1,0:T(8,128)S(1)}, u32[]{:S(2)}, u32[]{:S(2)}) %all-to-all-start.1) | async-done | bytes 3145760 | tf_op jit(solution)/shard_map/all_to_all | solution.py:30
  47.7 9.2 %all-to-all-start = ((f32[64,8,3072]{2,1,0:T(8,128)}), f32[64,8,3072]{2,1,0:T(8,128)}, u32[]{:S(2)}, u32[]{:S(2)}) async-start(f32[64,8,3072]{2,1,0:T(8,128)} %bitcast.52), calls=%async_computation | async-start | bytes 12582912 | tf_op jit(solution)/shard_map/all_to_all | solution.py:40
  57.6 5.8 %collective-permute-done = f32[8,64,1536]{2,1,0:T(8,128)} collective-permute-done((f32[8,64,1536]{2,1,0:T(8,128)S(1)}, f32[8,64,1536]{2,1,0:T(8,128)}, u32[]{:S(2)}, u32[]{:S(2)}) %collective-permute-start) | collective-permute-done | bytes 3145760 | tf_op jit(solution)/shard_map/ppermute | solution.py:31
  63.4 4.2 %select_bitcast_fusion = (f32[8,64,1,1536]{3,1,0,2:T(8,128)S(1)}, f32[8,64,1536]{2,1,0:T(8,128)}) fusion(f32[8,64,1536]{2,1,0:T(8,128)S(1)} %all-to-all-done.1, f32[8,64,1536]{2,1,0:T(8,128)} %collective-permute-done, pred[]{:T(512)S(6)} %eq.3), kind=kLoop, calls=%fused_computation.6 | loop fusion | flops 1572864 | bytes 12582913 | tf_op jit(solution)/shard_map/stack | solution.py:33
  67.6 4.9 %copy.14 = f32[8,64,1,1536]{3,2,1,0:T(1,128)} copy(f32[8,64,1,1536]{3,1,0,2:T(8,128)S(1)} %get-tuple-element.7) | data formatting | bytes 6291456 | tf_op jit(solution)/shard_map/stack | solution.py:33
  72.5 3.8 %stack.10 = f32[8,64,1,1536]{3,2,1,0:T(1,128)} reshape(f32[8,64,1536]{2,1,0:T(8,128)S(1)} %copy-done.1) | data formatting | bytes 6291456 | tf_op jit(solution)/shard_map/stack | solution.py:33
  76.3 11.2 %pad_maximum_fusion = f32[8,64,2,1536]{3,2,1,0:T(2,128)} fusion(f32[8,64,1,1536]{3,2,1,0:T(1,128)} %stack.10, f32[8,64,1,1536]{3,2,1,0:T(1,128)} %copy.14), kind=kLoop, calls=%fused_computation | loop fusion | flops 1572864 | bytes 12582912 | tf_op jit(solution)/shard_map/stack | solution.py:33
  87.5 9.1 %reshape.49 = f32[8,2,32,3072]{3,2,1,0:T(8,128)} reshape(f32[8,64,2,1536]{3,2,1,0:T(2,128)} %pad_maximum_fusion) | data formatting | bytes 12582912 | tf_op jit(solution)/shard_map/reshape | solution.py:34
  96.7 6.3 %copy.15 = f32[2,8,32,3072]{3,2,1,0:T(8,128)} copy(f32[2,8,32,3072]{3,2,0,1:T(8,128)} %bitcast.48) | data formatting | bytes 12582912 | tf_op jit(solution)/shard_map/transpose | solution.py:35
  103.7 2.7 fusion.12
  106.5 32.2 %all-to-all-done = f32[64,8,3072]{2,1,0:T(8,128)} async-done(((f32[64,8,3072]{2,1,0:T(8,128)}), f32[64,8,3072]{2,1,0:T(8,128)}, u32[]{:S(2)}, u32[]{:S(2)}) %all-to-all-start) | async-done | bytes 6291488 | tf_op jit(solution)/shard_map/all_to_all | solution.py:40
  138.7 9.1 %fusion.2 = f32[64,8,512]{2,1,0:T(8,128)S(1)} fusion(f32[512,3072]{1,0:T(8,128)} %bitcast.56, f32[64,8,3072]{2,1,0:T(8,128)} %all-to-all-done), kind=kOutput, calls=%fused_computation.8 | convolution fusion | flops 4831838208 | bytes 13631488 | tf_op jit(solution)/shard_map/dot_general | solution.py:11
  147.9 35.5 %all_to_all.25 = f32[64,8,640]{2,1,0:T(8,128)S(1)} all-to-all(f32[64,8,640]{2,1,0:T(8,128)S(1)} %pad_maximum_fusion.2), channel_id=1, replica_groups=mesh['block'=8,'core'=2,'col'=8] {'block','col'}, dimensions={0} | all-to-all | bytes 2621440 | tf_op jit(solution)/shard_map/all_to_all | solution.py:45
  183.6 25.1 %all_to_all.26 = f32[64,8,640]{2,1,0:T(8,128)S(1)} all-to-all(f32[64,8,640]{2,1,0:T(8,128)S(1)} %broadcast_in_dim.2), channel_id=1, replica_groups=mesh['block'=8,'core'=2,'col'=8] {'block','col'}, dimensions={0} | all-to-all | bytes 2621440 | tf_op jit(solution)/shard_map/all_to_all | solution.py:48
  211.2 11.5 %bitcast_subtract_fusion = f32[512,3072]{1,0:T(8,128)} fusion(f32[64,8,3072]{2,1,0:T(8,128)} %all-to-all-done, f32[512,3072]{1,0:T(8,128)} %bitcast.57, f32[512,256]{0,1:T(8,128)S(1)} %fusion.13, f32[512,256]{0,1:T(8,128)S(1)} %fusion.8), kind=kOutput, calls=%fused_computation.1 | convolution fusion | flops 4833673216 | bytes 19922944 | tf_op jit(solution)/shard_map/dot_general | solution.py:11
  222.7 9.1 %reshape.55 = f32[8,64,2,1536]{3,2,1,0:T(2,128)} reshape(f32[512,3072]{1,0:T(8,128)} %bitcast_subtract_fusion) | data formatting | bytes 12582912 | tf_op jit(solution)/shard_map/reshape | solution.py:57
  231.8 4.0 %copy.16 = f32[8,64,2,1536]{3,1,0,2:T(8,128)S(1)} copy(f32[8,64,2,1536]{3,2,1,0:T(2,128)} %reshape.55) | data formatting | bytes 12582912 | tf_op jit(solution)/shard_map/reshape | solution.py:57
  235.8 75.4 %all_to_all.27 = f32[16,64,1536]{2,1,0:T(8,128)S(1)} all-to-all(f32[16,64,1536]{2,1,0:T(8,128)S(1)} %bitcast.53), channel_id=1, replica_groups=mesh['block'=8,'core'=2,'col'=8] {'core','col'}, dimensions={0} | all-to-all | bytes 12582912 | tf_op jit(solution)/shard_map/all_to_all | solution.py:59
  311.2 3.6 %copy.17 = f32[2,64,8,1536]{3,2,1,0:T(8,128)S(1)} copy(f32[2,64,8,1536]{3,1,2,0:T(8,128)S(1)} %bitcast.54) | data formatting | bytes 12582912 | tf_op jit(solution)/shard_map/transpose | solution.py:60
  314.8 7.6 %copy.19 = f32[16,8,8,1536]{3,1,2,0:T(8,128)} copy(f32[16,8,8,1536]{3,2,1,0:T(8,128)S(1)} %bitcast.55) | data formatting | bytes 12582912
  (22 shorter events, 4.1 us)
Async XLA Ops:
  0.0 208.8 %copy-start = (f32[256,256]{1,0:T(8,128)S(1)}, f32[256,256]{1,0:T(8,128)}, u32[]{:S(2)}) copy-start(f32[256,256]{1,0:T(8,128)} %param.8) | copy-start | bytes 786436
  4.1 43.7 %all-to-all-start.1 = ((f32[8,64,1536]{2,1,0:T(8,128)}), f32[8,64,1536]{2,1,0:T(8,128)S(1)}, u32[]{:S(2)}, u32[]{:S(2)}) async-start(f32[8,64,1536]{2,1,0:T(8,128)} %bitcast.47), calls=%async_computation.1 | async-start | bytes 6291456 | tf_op jit(solution)/shard_map/all_to_all | solution.py:30
  47.7 91.0 %all-to-all-start = ((f32[64,8,3072]{2,1,0:T(8,128)}), f32[64,8,3072]{2,1,0:T(8,128)}, u32[]{:S(2)}, u32[]{:S(2)}) async-start(f32[64,8,3072]{2,1,0:T(8,128)} %bitcast.52), calls=%async_computation | async-start | bytes 12582912 | tf_op jit(solution)/shard_map/all_to_all | solution.py:40
  57.0 6.4 %collective-permute-start = (f32[8,64,1536]{2,1,0:T(8,128)S(1)}, f32[8,64,1536]{2,1,0:T(8,128)}, u32[]{:S(2)}, u32[]{:S(2)}) collective-permute-start(f32[8,64,1536]{2,1,0:T(8,128)S(1)} %all-to-all-done.1), channel_id=1, source_target_pairs={{0,8},{8,0},{1,9},{9,1},{2,10},{10,2},{3,11},{11,3},{4,12},{12,4},... | collective-permute-start | bytes 9437192 | tf_op jit(solution)/shard_map/ppermute | solution.py:31
  67.6 4.9 %copy-start.1 = (f32[8,64,1536]{2,1,0:T(8,128)S(1)}, f32[8,64,1536]{2,1,0:T(8,128)}, u32[]{:S(2)}) copy-start(f32[8,64,1536]{2,1,0:T(8,128)} %get-tuple-element.8) | copy-start | bytes 9437188
  96.7 6.3 %slice-start = ((s8[6291456]{0:T(1024)(128)(4,1)}), s8[4194304]{0:T(1024)(128)(4,1)S(1)}, s32[]{:S(2)}) async-start(s8[6291456]{0:T(1024)(128)(4,1)} %bitcast.49), calls=%async_computation.5 | async-start | bytes 8388608
  96.7 6.3 %slice-start.1 = ((s8[6291456]{0:T(1024)(128)(4,1)}), s8[2097152]{0:T(1024)(128)(4,1)S(1)}, s32[]{:S(2)}) async-start(s8[6291456]{0:T(1024)(128)(4,1)} %bitcast.49), calls=%async_computation.6 | async-start | bytes 4194304
  183.6 26.9 %copy-start.2 = (f32[256,256]{1,0:T(8,128)S(1)}, f32[256,256]{1,0:T(8,128)}, u32[]{:S(2)}) copy-start(f32[256,256]{1,0:T(8,128)} %param.9) | copy-start | bytes 786436

commit v2 on v1

v2 whole, which is shorter than its diff:
```python
import jax
import jax.numpy as jnp
from jax import lax
from jax.experimental import pallas as pl
from jax.experimental.pallas import tpu as pltpu
from jax.sharding import Mesh, PartitionSpec as P

CHIPS = ("block", "half", "place")
INNER = ("core", "half", "place")
CORES = 2
HALVES = 2
VMEM_LIMIT = 48 * 1024 * 1024
ANY = pl.BlockSpec(memory_space=pl.ANY)
SCALAR = pl.BlockSpec(memory_space=pltpu.SMEM)


def f32(*shape):
    return jax.ShapeDtypeStruct(shape, jnp.float32)


def params():
    return pltpu.CompilerParams(vmem_limit_bytes=VMEM_LIMIT)


def in_two(values):
    high = values.astype(jnp.bfloat16)
    return high, (values - high.astype(jnp.float32)).astype(jnp.bfloat16)


def dot3(left, right, right_dim):
    (lh, ll), (rh, rl) = left, right

    def dot(a, b):
        return lax.dot_general(
            a, b, (((1,), (right_dim,)), ((), ())), preferred_element_type=jnp.float32
        )

    return dot(lh, rh) + (dot(lh, rl) + dot(ll, rh))


def dot(left, right, left_dim, right_dim):
    return lax.dot_general(
        left,
        right,
        (((left_dim,), (right_dim,)), ((), ())),
        precision=lax.Precision.HIGHEST,
        preferred_element_type=jnp.float32,
    )


def copy_all(copies):
    for one in copies:
        one.start()
    for one in copies:
        one.wait()


def partner(place, j, core, half):
    return place ^ j ^ (2 * (core ^ half))


def times(index, size):
    return pl.ds(pl.multiple_of(index * size, size), size)


def pack_panels(where, first, second, order):
    held, rows = first.shape
    places = len(order)
    part = rows // places

    def kernel(where_ref, first_ref, second_ref, *rest):
        outs, sems = rest[:places], rest[places]
        copies = []
        for i, j in enumerate(order):
            at = times(partner(where_ref[2], j, where_ref[0], where_ref[1]), part)
            for p, ref in enumerate((first_ref, second_ref)):
                target = outs[i].at[pl.ds(p * held, held)]
                copies.append(pltpu.make_async_copy(ref.at[:, at], target, sems.at[2 * i + p]))
        copy_all(copies)

    return pl.pallas_call(
        kernel,
        out_shape=[f32(2 * held, part)] * places,
        in_specs=[SCALAR, ANY, ANY],
        out_specs=[ANY] * places,
        scratch_shapes=[pltpu.SemaphoreType.DMA((2 * places,))],
        compiler_params=params(),
        name="pack_panels",
    )(where, first, second)


def join_panels(where, pieces, order):
    places = len(order)
    held, part = pieces[0].shape[0] // 2, pieces[0].shape[1]

    def kernel(where_ref, *rest):
        ins, out, sems = rest[:places], rest[places], rest[places + 1]
        copies = []
        for i, j in enumerate(order):
            at = times(partner(where_ref[2], j, where_ref[0], where_ref[1]), held)
            for p in range(2):
                source = ins[i].at[pl.ds(p * held, held)]
                copies.append(pltpu.make_async_copy(source, out.at[p, at], sems.at[2 * i + p]))
        copy_all(copies)

    return pl.pallas_call(
        kernel,
        out_shape=f32(2, places * held, part),
        in_specs=[SCALAR] + [ANY] * places,
        out_specs=ANY,
        scratch_shapes=[pltpu.SemaphoreType.DMA((2 * places,))],
        compiler_params=params(),
        name="join_panels",
    )(where, *pieces)


def prepare(where, own, other, chips, held):
    _, count, rows = own.shape
    width = CORES * count
    steps = 6
    tile = rows // steps

    def kernel(where_ref, own_ref, other_ref, high_ref, low_ref, out_ref, overlap_ref):
        step = pl.program_id(0)

        @pl.when(step == 0)
        def _():
            overlap_ref[...] = jnp.zeros_like(overlap_ref)

        for p in range(2):
            for d, ref in enumerate((own_ref, other_ref)):
                at = times(p * CORES + (where_ref[0] ^ d), count)
                high_ref[at], low_ref[at] = in_two(ref[p])
        first, second = ((high_ref[at], low_ref[at]) for at in (pl.ds(0, width), pl.ds(width, width)))
        overlap_ref[...] += dot3(first, second, 1)

        @pl.when(step == steps - 1)
        def _():
            half = chips // 2
            out_ref[:half] = overlap_ref[:, :count].reshape(half, held, count)
            out_ref[half:] = overlap_ref[:, count:].reshape(half, held, count)

    panels = pl.BlockSpec((2, count, tile), lambda i, w: (0, 0, i))
    part = pl.BlockSpec((2 * width, tile), lambda i, w: (0, i))
    bf16 = jax.ShapeDtypeStruct((2 * width, rows), jnp.bfloat16)
    return pl.pallas_call(
        kernel,
        out_shape=[bf16, bf16, f32(chips, held, count)],
        grid_spec=pltpu.PrefetchScalarGridSpec(
            num_scalar_prefetch=1,
            grid=(steps,),
            in_specs=[panels, panels],
            out_specs=[part, part, pl.BlockSpec((chips, held, count), lambda i, w: (0, 0, 0))],
            scratch_shapes=[pltpu.VMEM((width, width), jnp.float32)],
        ),
        compiler_params=params(),
        name="prepare",
    )(where, own, other)


def project(zt, high, low, overlap):
    vectors, rows = zt.shape
    both = high.shape[0]
    chips, held, more = overlap.shape
    steps = 6
    tile = rows // steps

    def kernel(z_ref, high_ref, low_ref, overlap_ref, out_ref, sum_ref):
        step = pl.program_id(0)

        @pl.when(step == 0)
        def _():
            sum_ref[...] = jnp.zeros_like(sum_ref)

        sum_ref[...] += dot3(in_two(z_ref[...]), (high_ref[...], low_ref[...]), 1)

        @pl.when(step == steps - 1)
        def _():
            out_ref[:, :, :both] = sum_ref[...].reshape(chips, held, both)
            out_ref[:, :, both:] = overlap_ref[...]

    tiles = pl.BlockSpec((both, tile), lambda i: (0, i))
    return pl.pallas_call(
        kernel,
        out_shape=f32(chips, held, both + more),
        grid=(steps,),
        in_specs=[
            pl.BlockSpec((vectors, tile), lambda i: (0, i)),
            tiles,
            tiles,
            pl.BlockSpec((chips, held, more), lambda i: (0, 0, 0)),
        ],
        out_specs=pl.BlockSpec((chips, held, both + more), lambda i: (0, 0, 0)),
        scratch_shapes=[pltpu.VMEM((vectors, both), jnp.float32)],
        compiler_params=params(),
        name="project",
    )(zt, high, low, overlap)


def update(where, zt, weights, high, low, flip, order):
    vectors, rows = zt.shape
    both = high.shape[0]
    places = len(order)
    block = vectors // (HALVES * places)
    steps = 6
    tile = rows // steps

    def target(w, j):
        return (w[0] ^ flip) * places + partner(w[2], j, w[0], w[1])

    def kernel(where_ref, *refs):
        z_refs, (weights_ref, high_ref, low_ref), outs = refs[:places], refs[places:-places], refs[-places:]
        rows = [weights_ref[times(target(where_ref, j), block)] for j in order]
        change = dot3(in_two(jnp.concatenate(rows, axis=0)), (high_ref[...], low_ref[...]), 0)
        for i in range(places):
            outs[i][...] = z_refs[i][...] - change[i * block : (i + 1) * block]

    def z_spec(j):
        return pl.BlockSpec((block, tile), lambda i, w: (target(w, j), i))

    tiles = pl.BlockSpec((both, tile), lambda i, w: (0, i))
    return pl.pallas_call(
        kernel,
        out_shape=[f32(block, rows)] * places,
        grid_spec=pltpu.PrefetchScalarGridSpec(
            num_scalar_prefetch=1,
            grid=(steps,),
            in_specs=[z_spec(j) for j in order]
            + [pl.BlockSpec((vectors, both), lambda i, w: (0, 0)), tiles, tiles],
            out_specs=[pl.BlockSpec((block, tile), lambda i, w: (0, i))] * places,
        ),
        compiler_params=params(),
        name="update",
    )(where, *[zt] * places, weights, high, low)


def gather(where, pieces, names, places, out=None):
    block, part = pieces[0].shape
    n = len(pieces)

    def kernel(where_ref, *refs):
        ins, dst, sems = refs[:n], refs[-2], refs[-1]
        copies = []
        for i, (flip, j) in enumerate(names):
            core = where_ref[1] ^ flip
            target = dst.at[times(core, block), times(partner(where_ref[2], j, where_ref[0], core), part)]
            copies.append(pltpu.make_async_copy(ins[i], target, sems.at[i]))
        copy_all(copies)

    held = [] if out is None else [out]
    return pl.pallas_call(
        kernel,
        out_shape=f32(CORES * block, places * part),
        in_specs=[SCALAR] + [ANY] * (n + len(held)),
        out_specs=ANY,
        scratch_shapes=[pltpu.SemaphoreType.DMA((n,))],
        input_output_aliases={n + 1: 0} if held else {},
        compiler_params=params(),
        name="gather",
    )(where, *pieces, *held)


def body(vectors_in, panel_first, panel_second, factor_first, factor_second):
    blocks, places = lax.axis_size("block"), lax.axis_size("place")
    chips = blocks * HALVES * places
    held = vectors_in.shape[0]
    width = panel_first.shape[1] * HALVES * places
    where = jnp.stack([lax.axis_index(name) for name in INNER]).astype(jnp.int32)

    def permute(piece, target):
        index = [(c, h, p) for c in range(CORES) for h in range(HALVES) for p in range(places)]
        return lax.ppermute(piece, INNER, [(i, index.index(target(*at))) for i, at in enumerate(index)])

    order = (3, 1, 0, 2)
    pieces = pack_panels(where, panel_first.T, panel_second.T, order)
    pieces = [
        permute(piece, lambda c, h, p: (h, c, partner(p, j, c, h))) for j, piece in zip(order, pieces)
    ]
    vectors_in, pieces = lax.optimization_barrier((vectors_in, pieces))
    zt = lax.all_to_all(vectors_in, CHIPS, split_axis=1, concat_axis=0, tiled=True)
    own = join_panels(where, pieces, order)
    other = lax.ppermute(own, "core", [(0, 1), (1, 0)])
    high, low, overlap = prepare(where, own, other, chips, held)

    partial = project(zt, high, low, overlap)
    parts = lax.all_to_all(partial, CHIPS, split_axis=0, concat_axis=0, tiled=True)
    total = jnp.sum(parts, axis=0)
    copies = jnp.broadcast_to(total[None], (chips,) + total.shape)
    total = lax.all_to_all(copies, CHIPS, split_axis=0, concat_axis=0, tiled=True)
    overlap = total[:, :, 2 * width :].reshape(2, width, -1)
    overlap = jnp.concatenate([overlap[0], overlap[1]], axis=1)
    total = total.reshape(chips * held, -1)
    first = dot(total[:, :width], factor_first, 1, 1)
    second = total[:, width : 2 * width] - dot(first, overlap, 1, 0)
    second = dot(second, factor_second, 1, 1)
    weights = jnp.concatenate([first, second], axis=1)

    out = None
    for flip in range(HALVES):
        pieces = update(where, zt, weights, high, low, flip, order)
        pieces = [
            permute(piece, lambda c, h, p: (h, c ^ flip, partner(p, j, c, h)))
            for j, piece in zip(order, pieces)
        ]
        out = gather(where, pieces, [(flip, j) for j in order], places, out)
    return out


def solution(mesh):
    rows, cols = mesh.devices.shape
    blocks, places = rows // CORES, cols // HALVES
    split = Mesh(mesh.devices.reshape(blocks, CORES, HALVES, places), ("block",) + INNER)
    row, col = ("block", "core"), ("half", "place")
    return jax.shard_map(
        body,
        mesh=split,
        in_specs=(P(row + col, None), P(row, col), P(row, col), P(), P()),
        out_specs=P(col, row),
        check_vma=False,
    )
```

time: 327 us -> 295 us (0.902); the launches traced: 323 us -> 295 us
  waiting for transfers between devices: 69.1 us -> 161 us
  blocking collectives: 136 us -> 59.4 us
  local copies, waits for them, and re-layouts: 57.5 us -> 5.06 us
  Pallas kernels: 0 us -> 40.8 us
  matrix products: 25.6 us -> 2.27 us
  other arithmetic: 17.8 us -> 1.62 us
  starting transfers between devices: 16.2 us -> 24.5 us
    ppermute x0 -> x12, waiting for transfers between devices: none -> 92.4 us  [permute(): lax.ppermute(piece, INNER, [(i, index.index(target(*at))) for i, at in en...]
    all_to_all x1 -> x0, blocking collectives: 75.4 us -> none  [body(): lax.all_to_all(zt, ('core', 'col'), split_axis=0, concat_axis=0, tiled=True)]
    pallas_call x0 -> x8, Pallas kernels: none -> 40.8 us  [the longest x2 15.3 us: update(): pl.pallas_call(kernel, out_shape=[f32(block, rows)] * places, grid_spec=p...]
    reshape x6 -> x0, local copies, waits for them, and re-layouts: 24.3 us -> none  [the longest x2 13.1 us: body(): zt = zt.reshape(blocks, cols * held, CORES, part).transpose(2, 0, 1, 3)]
    dot_general x6 -> x3, matrix products: 25.6 us -> 2.27 us  [dot(): lax.dot_general(left, right, (((left_dim,), (right_dim,)), ((), ())), pre...]
    transpose x3 -> x0, local copies, waits for them, and re-layouts: 16.1 us -> none  [the longest x1 6.33 us: body(): panels = panels.transpose(1, 0, 2, 3).reshape(2 * width, CORES * part)]
    another operation x2 -> x1, other arithmetic: 15.5 us -> 0.08 us  [body(): jnp.stack([lax.axis_index(name) for name in INNER]).astype(jnp.int32)]
    ppermute x0 -> x12, starting transfers between devices: none -> 15.1 us  [permute(): lax.ppermute(piece, INNER, [(i, index.index(target(*at))) for i, at in en...]
  transfers between devices with their start and end apart: 3 -> 14, of which waited for: 3 -> 6; matrix products, arithmetic and copies ran while one was open for 15% -> 0% of each run, Pallas kernels for 0% -> 7%
where the time goes in v2:
time: 295 us
  waiting for transfers between devices  161 us (55%)
  blocking collectives  59.4 us (20%)
  Pallas kernels  40.8 us (14%)
  starting transfers between devices  24.5 us (8%)
  local copies, waits for them, and re-layouts  5.06 us (2%)
    ppermute x12, waiting for transfers between devices, permute(): lax.ppermute(piece, INNER, [(i, index.index(target(*at))) for i, at in en...  92.4 us
    all_to_all x1, waiting for transfers between devices, body(): lax.all_to_all(vectors_in, CHIPS, split_axis=1, concat_axis=0, tiled=True)  62.4 us
    all_to_all x1, blocking collectives, body(): lax.all_to_all(partial, CHIPS, split_axis=0, concat_axis=0, tiled=True)  34.6 us
    all_to_all x1, blocking collectives, body(): lax.all_to_all(copies, CHIPS, split_axis=0, concat_axis=0, tiled=True)  24.8 us
    pallas_call x2, Pallas kernels, update(): pl.pallas_call(kernel, out_shape=[f32(block, rows)] * places, grid_spec=p...  15.3 us
    ppermute x12, starting transfers between devices, permute(): lax.ppermute(piece, INNER, [(i, index.index(target(*at))) for i, at in en...  15.1 us
    all_to_all x1, starting transfers between devices, body(): lax.all_to_all(vectors_in, CHIPS, split_axis=1, concat_axis=0, tiled=True)  9.31 us
    pallas_call x1, Pallas kernels, project(): pl.pallas_call(kernel, out_shape=f32(chips, held, both + more), grid=(ste...  8.52 us
  transfers between devices with their start and end apart: 14, of which 6 were waited for; matrix products, arithmetic and copies ran while one was open for 0% of the time, Pallas kernels for 7%

profile of v2, /device:TPU:0, one launch (start us, length us, event | category | flops | bytes accessed | tf_op | source)
XLA Modules:
  0.0 294.6 jit_solution(17025307349207912092)
XLA Ops:
  0.1 1.4 copy-done.2
  1.5 2.1 pack_panels.1
  3.6 4.2 %collective-permute-start = (f32[64,3072]{1,0:T(8,128)S(1)}, f32[64,3072]{1,0:T(8,128)S(1)}, u32[]{:S(2)}, u32[]{:S(2)}) collective-permute-start(f32[64,3072]{1,0:T(8,128)S(1)} %get-tuple-element.25), channel_id=1, source_target_pairs={{0,3},{1,2},{2,1},{3,0},{4,9},{5,8},{6,11},{7,10},{8,5},{9,4},{10,... | collective-permute-start | bytes 2359304 | tf_op jit(solution)/shard_map/ppermute | solution.py:272
  8.5 1.6 collective-permute-start.3
  10.1 32.4 %collective-permute-done.rest_0_ = f32[64,3072]{1,0:T(8,128)S(1)} collective-permute-done((f32[64,3072]{1,0:T(8,128)S(1)}, f32[64,3072]{1,0:T(8,128)S(1)}, u32[]{:S(2)}, u32[]{:S(2)}) %collective-permute-start) | collective-permute-done | bytes 786464 | tf_op jit(solution)/shard_map/ppermute | solution.py:272
  42.6 2.0 collective-permute-done.3.rest_3_
  44.6 9.3 %all-to-all-start = ((f32[8,64,3072]{2,0,1:T(8,128)}), f32[8,64,3072]{2,0,1:T(8,128)}, u32[]{:S(2)}, u32[]{:S(2)}) async-start(f32[8,64,3072]{2,0,1:T(8,128)} %bitcast.19), calls=%async_computation | async-start | bytes 12582912 | tf_op jit(solution)/shard_map/all_to_all | solution.py:280
  53.9 2.3 join_panels.1.own_ref
  56.3 5.9 %collective-permute-done.4.other_ref = f32[2,128,3072]{2,1,0:T(8,128)S(1)} collective-permute-done((f32[2,128,3072]{2,1,0:T(8,128)}, f32[2,128,3072]{2,1,0:T(8,128)S(1)}, u32[]{:S(2)}, u32[]{:S(2)}) %collective-permute-start.4) | collective-permute-done | bytes 3145760 | tf_op jit(solution)/shard_map/ppermute | solution.py:282
  62.1 1.7 copy-done.5
  63.8 8.2 %prepare.1 = (bf16[512,3072]{1,0:T(8,128)(2,1)S(1)}, bf16[512,3072]{1,0:T(8,128)(2,1)}, f32[64,8,128]{2,1,0:T(8,128)S(1)}) custom-call(s32[3]{0:T(128)S(1)} %pad_add_fusion.where_ref, f32[2,128,3072]{2,1,0:T(8,128)} %join_panels.1.own_ref, f32[2,128,3072]{2,1,0:T(8,128)} %copy-done.5), custom_call_target="tpu_custom_call" | custom-call | tf_op jit(solution)/shard_map/prepare/pallas_call | solution.py:146
  72.7 62.4 %all-to-all-done = f32[8,64,3072]{2,0,1:T(8,128)} async-done(((f32[8,64,3072]{2,0,1:T(8,128)}), f32[8,64,3072]{2,0,1:T(8,128)}, u32[]{:S(2)}, u32[]{:S(2)}) %all-to-all-start) | async-done | bytes 6291488 | tf_op jit(solution)/shard_map/all_to_all | solution.py:280
  136.0 8.5 %project.1 = f32[64,8,640]{2,1,0:T(8,128)S(1)} custom-call(f32[512,3072]{1,0:T(8,128)} %bitcast.7.z_ref.refs_0_.refs_1_.refs_2_.refs_3_, bf16[512,3072]{1,0:T(8,128)(2,1)S(1)} %get-tuple-element.34.high_ref.refs_5_, bf16[512,3072]{1,0:T(8,128)(2,1)} %get-tuple-element.35.low_ref.refs_6_, f32[64,8,128]{2,1,0:T(8,128)S(1)} %copy-done.4), custom_call_target="tpu_custom_call" | custom-call | tf_op jit(solution)/shard_map/project/pallas_call | solution.py:183
  144.6 34.6 %all_to_all.29 = f32[64,8,640]{2,1,0:T(8,128)} all-to-all(f32[64,8,640]{2,1,0:T(8,128)S(1)} %project.1), channel_id=1, replica_groups=mesh['block'=8,'core'=2,'half'=2,'place'=4] {'block','half','place'}, dimensions={0} | all-to-all | bytes 2621440 | tf_op jit(solution)/shard_map/all_to_all | solution.py:286
  179.2 1.4 reduce_sum.9
  180.7 24.8 %all_to_all.30 = f32[64,8,640]{2,1,0:T(8,128)S(1)} all-to-all(f32[64,8,640]{2,1,0:T(8,128)S(1)} %broadcast_in_dim.2), channel_id=1, replica_groups=mesh['block'=8,'core'=2,'half'=2,'place'=4] {'block','half','place'}, dimensions={0} | all-to-all | bytes 2621440 | tf_op jit(solution)/shard_map/all_to_all | solution.py:289
  208.2 7.7 %update.3 = (f32[64,3072]{1,0:T(8,128)S(1)}, f32[64,3072]{1,0:T(8,128)S(1)}, f32[64,3072]{1,0:T(8,128)S(1)}, f32[64,3072]{1,0:T(8,128)S(1)}) custom-call(s32[3]{0:T(128)S(1)} %pad_add_fusion.where_ref, f32[512,3072]{1,0:T(8,128)} %bitcast.7.z_ref.refs_0_.refs_1_.refs_2_.refs_3_, f32[512,3072]{1,0:T(8,128)} %bitcast.7.z_ref.refs_0_.refs_1_.refs_2_.refs_3_, ...), custom_call_target="tpu_custom_call" | custom-call | tf_op jit(solution)/shard_map/update/pallas_call | solution.py:222
  217.9 7.7 %update.2 = (f32[64,3072]{1,0:T(8,128)S(1)}, f32[64,3072]{1,0:T(8,128)S(1)}, f32[64,3072]{1,0:T(8,128)S(1)}, f32[64,3072]{1,0:T(8,128)S(1)}) custom-call(s32[3]{0:T(128)S(1)} %pad_add_fusion.where_ref, f32[512,3072]{1,0:T(8,128)} %bitcast.7.z_ref.refs_0_.refs_1_.refs_2_.refs_3_, f32[512,3072]{1,0:T(8,128)} %bitcast.7.z_ref.refs_0_.refs_1_.refs_2_.refs_3_, ...), custom_call_target="tpu_custom_call" | custom-call | tf_op jit(solution)/shard_map/update/pallas_call | solution.py:222
  225.6 5.3 %collective-permute-start.5 = (f32[64,3072]{1,0:T(8,128)S(1)}, f32[64,3072]{1,0:T(8,128)S(1)}, u32[]{:S(2)}, u32[]{:S(2)}) collective-permute-start(f32[64,3072]{1,0:T(8,128)S(1)} %get-tuple-element.37), channel_id=1, source_target_pairs={{0,7},{1,6},{2,5},{3,4},{4,13},{5,12},{6,15},{7,14},{8,1},{9,0},{1... | collective-permute-start | bytes 2359304 | tf_op jit(solution)/shard_map/ppermute | solution.py:272
  230.9 25.9 %collective-permute-done.9.refs_0_ = f32[64,3072]{1,0:T(8,128)S(1)} collective-permute-done((f32[64,3072]{1,0:T(8,128)S(1)}, f32[64,3072]{1,0:T(8,128)S(1)}, u32[]{:S(2)}, u32[]{:S(2)}) %collective-permute-start.9) | collective-permute-done | bytes 786464 | tf_op jit(solution)/shard_map/ppermute | solution.py:272
  256.8 1.2 collective-permute-start.8
  258.0 32.1 %collective-permute-done.12.refs_3_ = f32[64,3072]{1,0:T(8,128)S(1)} collective-permute-done((f32[64,3072]{1,0:T(8,128)S(1)}, f32[64,3072]{1,0:T(8,128)S(1)}, u32[]{:S(2)}, u32[]{:S(2)}) %collective-permute-start.12) | collective-permute-done | bytes 786464 | tf_op jit(solution)/shard_map/ppermute | solution.py:272
  290.1 2.2 gather.2.refs_4_
  292.4 2.2 gather.3
  (37 shorter events, 7.3 us)
Async XLA Ops:
  0.0 205.5 %copy-start = (f32[256,256]{1,0:T(8,128)S(1)}, f32[256,256]{1,0:T(8,128)}, u32[]{:S(2)}) copy-start(f32[256,256]{1,0:T(8,128)} %param.8) | copy-start | bytes 786436
  0.1 1.4 copy-start.2
  3.6 39.0 %collective-permute-start = (f32[64,3072]{1,0:T(8,128)S(1)}, f32[64,3072]{1,0:T(8,128)S(1)}, u32[]{:S(2)}, u32[]{:S(2)}) collective-permute-start(f32[64,3072]{1,0:T(8,128)S(1)} %get-tuple-element.25), channel_id=1, source_target_pairs={{0,3},{1,2},{2,1},{3,0},{4,9},{5,8},{6,11},{7,10},{8,5},{9,4},{10,... | collective-permute-start | bytes 2359304 | tf_op jit(solution)/shard_map/ppermute | solution.py:272
  7.8 34.8 %collective-permute-start.1 = (f32[64,3072]{1,0:T(8,128)S(1)}, f32[64,3072]{1,0:T(8,128)S(1)}, u32[]{:S(2)}, u32[]{:S(2)}) collective-permute-start(f32[64,3072]{1,0:T(8,128)S(1)} %get-tuple-element.26), channel_id=1, source_target_pairs={{0,1},{1,0},{2,3},{3,2},{4,11},{5,10},{6,9},{7,8},{8,7},{9,6},{10,... | collective-permute-start | bytes 2359304 | tf_op jit(solution)/shard_map/ppermute | solution.py:272
  7.8 34.8 %collective-permute-start.2 = (f32[64,3072]{1,0:T(8,128)S(1)}, f32[64,3072]{1,0:T(8,128)S(1)}, u32[]{:S(2)}, u32[]{:S(2)}) collective-permute-start(f32[64,3072]{1,0:T(8,128)S(1)} %get-tuple-element.27), channel_id=1, source_target_pairs={{0,0},{1,1},{2,2},{3,3},{4,10},{5,11},{6,8},{7,9},{8,6},{9,7},{10,... | collective-permute-start | bytes 2359304 | tf_op jit(solution)/shard_map/ppermute | solution.py:272
  8.5 36.1 %collective-permute-start.3 = (f32[64,3072]{1,0:T(8,128)S(1)}, f32[64,3072]{1,0:T(8,128)S(1)}, u32[]{:S(2)}, u32[]{:S(2)}) collective-permute-start(f32[64,3072]{1,0:T(8,128)S(1)} %get-tuple-element.28), channel_id=1, source_target_pairs={{0,2},{1,3},{2,0},{3,1},{4,8},{5,9},{6,10},{7,11},{8,4},{9,5},{10,... | collective-permute-start | bytes 2359304 | tf_op jit(solution)/shard_map/ppermute | solution.py:272
  44.6 90.5 %all-to-all-start = ((f32[8,64,3072]{2,0,1:T(8,128)}), f32[8,64,3072]{2,0,1:T(8,128)}, u32[]{:S(2)}, u32[]{:S(2)}) async-start(f32[8,64,3072]{2,0,1:T(8,128)} %bitcast.19), calls=%async_computation | async-start | bytes 12582912 | tf_op jit(solution)/shard_map/all_to_all | solution.py:280
  56.2 6.0 %collective-permute-start.4 = (f32[2,128,3072]{2,1,0:T(8,128)}, f32[2,128,3072]{2,1,0:T(8,128)S(1)}, u32[]{:S(2)}, u32[]{:S(2)}) collective-permute-start(f32[2,128,3072]{2,1,0:T(8,128)} %join_panels.1.own_ref), channel_id=1, source_target_pairs={{0,8},{8,0},{1,9},{9,1},{2,10},{10,2},{3,11},{11,3},{4,12},{12,4},... | collective-permute-start | bytes 9437192 | tf_op jit(solution)/shard_map/ppermute | solution.py:282
  62.1 1.7 copy-start.5
  72.0 0.7 copy-start.3
  72.7 71.9 %copy-start.1 = (bf16[512,3072]{1,0:T(8,128)(2,1)}, bf16[512,3072]{1,0:T(8,128)(2,1)S(1)}, u32[]{:S(2)}) copy-start(bf16[512,3072]{1,0:T(8,128)(2,1)S(1)} %get-tuple-element.34.high_ref.refs_5_) | copy-start | bytes 9437188
  135.1 1.0 copy-start.4
  206.2 1.3 copy-start.6
  215.9 41.0 %collective-permute-start.9 = (f32[64,3072]{1,0:T(8,128)S(1)}, f32[64,3072]{1,0:T(8,128)S(1)}, u32[]{:S(2)}, u32[]{:S(2)}) collective-permute-start(f32[64,3072]{1,0:T(8,128)S(1)} %get-tuple-element.41), channel_id=1, source_target_pairs={{0,3},{1,2},{2,1},{3,0},{4,9},{5,8},{6,11},{7,10},{8,5},{9,4},{10,... | collective-permute-start | bytes 2359304 | tf_op jit(solution)/shard_map/ppermute | solution.py:272
  216.8 40.0 %collective-permute-start.10 = (f32[64,3072]{1,0:T(8,128)S(1)}, f32[64,3072]{1,0:T(8,128)S(1)}, u32[]{:S(2)}, u32[]{:S(2)}) collective-permute-start(f32[64,3072]{1,0:T(8,128)S(1)} %get-tuple-element.42), channel_id=1, source_target_pairs={{0,1},{1,0},{2,3},{3,2},{4,11},{5,10},{6,9},{7,8},{8,7},{9,6},{10,... | collective-permute-start | bytes 2359304 | tf_op jit(solution)/shard_map/ppermute | solution.py:272
  217.2 39.6 %collective-permute-start.11 = (f32[64,3072]{1,0:T(8,128)S(1)}, f32[64,3072]{1,0:T(8,128)S(1)}, u32[]{:S(2)}, u32[]{:S(2)}) collective-permute-start(f32[64,3072]{1,0:T(8,128)S(1)} %get-tuple-element.43), channel_id=1, source_target_pairs={{0,0},{1,1},{2,2},{3,3},{4,10},{5,11},{6,8},{7,9},{8,6},{9,7},{10,... | collective-permute-start | bytes 2359304 | tf_op jit(solution)/shard_map/ppermute | solution.py:272
  225.6 66.7 %collective-permute-start.5 = (f32[64,3072]{1,0:T(8,128)S(1)}, f32[64,3072]{1,0:T(8,128)S(1)}, u32[]{:S(2)}, u32[]{:S(2)}) collective-permute-start(f32[64,3072]{1,0:T(8,128)S(1)} %get-tuple-element.37), channel_id=1, source_target_pairs={{0,7},{1,6},{2,5},{3,4},{4,13},{5,12},{6,15},{7,14},{8,1},{9,0},{1... | collective-permute-start | bytes 2359304 | tf_op jit(solution)/shard_map/ppermute | solution.py:272
  230.9 61.4 %collective-permute-start.6 = (f32[64,3072]{1,0:T(8,128)S(1)}, f32[64,3072]{1,0:T(8,128)S(1)}, u32[]{:S(2)}, u32[]{:S(2)}) collective-permute-start(f32[64,3072]{1,0:T(8,128)S(1)} %get-tuple-element.38), channel_id=1, source_target_pairs={{0,5},{1,4},{2,7},{3,6},{4,15},{5,14},{6,13},{7,12},{8,3},{9,2},{1... | collective-permute-start | bytes 2359304 | tf_op jit(solution)/shard_map/ppermute | solution.py:272
  256.8 33.3 %collective-permute-start.12 = (f32[64,3072]{1,0:T(8,128)S(1)}, f32[64,3072]{1,0:T(8,128)S(1)}, u32[]{:S(2)}, u32[]{:S(2)}) collective-permute-start(f32[64,3072]{1,0:T(8,128)S(1)} %get-tuple-element.44), channel_id=1, source_target_pairs={{0,2},{1,3},{2,0},{3,1},{4,8},{5,9},{6,10},{7,11},{8,4},{9,5},{10,... | collective-permute-start | bytes 2359304 | tf_op jit(solution)/shard_map/ppermute | solution.py:272
  256.8 35.5 %collective-permute-start.7 = (f32[64,3072]{1,0:T(8,128)S(1)}, f32[64,3072]{1,0:T(8,128)S(1)}, u32[]{:S(2)}, u32[]{:S(2)}) collective-permute-start(f32[64,3072]{1,0:T(8,128)S(1)} %get-tuple-element.39), channel_id=1, source_target_pairs={{0,4},{1,5},{2,6},{3,7},{4,14},{5,15},{6,12},{7,13},{8,2},{9,3},{1... | collective-permute-start | bytes 2359304 | tf_op jit(solution)/shard_map/ppermute | solution.py:272
  256.8 35.5 %collective-permute-start.8 = (f32[64,3072]{1,0:T(8,128)S(1)}, f32[64,3072]{1,0:T(8,128)S(1)}, u32[]{:S(2)}, u32[]{:S(2)}) collective-permute-start(f32[64,3072]{1,0:T(8,128)S(1)} %get-tuple-element.40), channel_id=1, source_target_pairs={{0,6},{1,7},{2,4},{3,5},{4,12},{5,13},{6,14},{7,15},{8,0},{9,1},{1... | collective-permute-start | bytes 2359304 | tf_op jit(solution)/shard_map/ppermute | solution.py:272

commit v3 on v2

v3 whole, which is shorter than its diff:
```python
import jax
import jax.numpy as jnp
from jax import lax
from jax.experimental import pallas as pl
from jax.experimental.pallas import tpu as pltpu
from jax.sharding import Mesh, PartitionSpec as P

CHIPS = ("block", "half", "place")
INNER = ("core", "half", "place")
CORES = 2
HALVES = 2
VMEM_LIMIT = 24 * 1024 * 1024
ANY = pl.BlockSpec(memory_space=pl.ANY)
WHOLE = pl.BlockSpec(memory_space=pltpu.VMEM)
SCALAR = pl.BlockSpec(memory_space=pltpu.SMEM)


def f32(*shape):
    return jax.ShapeDtypeStruct(shape, jnp.float32)


def params():
    return pltpu.CompilerParams(vmem_limit_bytes=VMEM_LIMIT)


def in_two(values):
    high = values.astype(jnp.bfloat16)
    return high, (values - high.astype(jnp.float32)).astype(jnp.bfloat16)


def dot3(left, right, right_dim):
    (lh, ll), (rh, rl) = left, right

    def dot(a, b):
        return lax.dot_general(
            a, b, (((1,), (right_dim,)), ((), ())), preferred_element_type=jnp.float32
        )

    return dot(lh, rh) + (dot(lh, rl) + dot(ll, rh))


def copy_all(copies):
    for one in copies:
        one.start()
    for one in copies:
        one.wait()


def partner(place, j, core, half):
    return place ^ j ^ (2 * (core ^ half))


def times(index, size):
    return pl.ds(pl.multiple_of(index * size, size), size)


def pack_panels(where, first, second, order, places):
    held, rows = first.shape
    part = rows // places
    count = len(order)

    def kernel(where_ref, *refs):
        for i, out in enumerate(refs[2 * count :]):
            out[:held] = refs[2 * i][...]
            out[held:] = refs[2 * i + 1][...]

    def spec(j):
        return pl.BlockSpec((held, part), lambda i, w: (0, partner(w[2], j, w[0], w[1])))

    return pl.pallas_call(
        kernel,
        out_shape=[f32(2 * held, part)] * count,
        grid_spec=pltpu.PrefetchScalarGridSpec(
            num_scalar_prefetch=1,
            grid=(1,),
            in_specs=[spec(j) for j in order for _ in range(2)],
            out_specs=[pl.BlockSpec((2 * held, part), lambda i, w: (0, 0))] * count,
        ),
        compiler_params=params(),
        name="pack_panels",
    )(where, *[first, second] * count)


def prepare(where, own, other, order, chips, held):
    places = len(order)
    held_cols, rows = own[0].shape[0] // 2, own[0].shape[1]
    count = places * held_cols
    width = CORES * count
    steps = 6
    tile = rows // steps

    def kernel(where_ref, *refs):
        ins, (high_ref, low_ref, out_ref, overlap_ref) = refs[: 2 * places], refs[2 * places :]
        step = pl.program_id(0)

        @pl.when(step == 0)
        def _():
            overlap_ref[...] = jnp.zeros_like(overlap_ref)

        for d in range(CORES):
            core = where_ref[0] ^ d
            for i, j in enumerate(order):
                place = partner(where_ref[2], j, core, where_ref[1])
                for p in range(2):
                    at = times((p * CORES + core) * places + place, held_cols)
                    values = ins[d * places + i][pl.ds(p * held_cols, held_cols)]
                    high_ref[at], low_ref[at] = in_two(values)
        first, second = ((high_ref[at], low_ref[at]) for at in (pl.ds(0, width), pl.ds(width, width)))
        overlap_ref[...] += dot3(first, second, 1)

        @pl.when(step == steps - 1)
        def _():
            half = chips // 2
            out_ref[:half] = overlap_ref[:, :count].reshape(half, held, count)
            out_ref[half:] = overlap_ref[:, count:].reshape(half, held, count)

    piece = pl.BlockSpec((2 * held_cols, tile), lambda i, w: (0, i))
    part = pl.BlockSpec((2 * width, tile), lambda i, w: (0, i))
    bf16 = jax.ShapeDtypeStruct((2 * width, rows), jnp.bfloat16)
    return pl.pallas_call(
        kernel,
        out_shape=[bf16, bf16, f32(chips, held, count)],
        grid_spec=pltpu.PrefetchScalarGridSpec(
            num_scalar_prefetch=1,
            grid=(steps,),
            in_specs=[piece] * (2 * places),
            out_specs=[part, part, pl.BlockSpec((chips, held, count), lambda i, w: (0, 0, 0))],
            scratch_shapes=[pltpu.VMEM((width, width), jnp.float32)],
        ),
        compiler_params=params(),
        name="prepare",
    )(where, *own, *other)


def project(zt, high, low, overlap):
    vectors, rows = zt.shape
    both = high.shape[0]
    chips, held, more = overlap.shape
    steps = 2

    def kernel(z_ref, high_ref, low_ref, overlap_ref, out_ref):
        sums = dot3(in_two(z_ref[...]), (high_ref[...], low_ref[...]), 1)
        out_ref[:, :, :both] = sums.reshape(chips // steps, held, both)
        out_ref[:, :, both:] = overlap_ref[...]

    return pl.pallas_call(
        kernel,
        out_shape=f32(chips, held, both + more),
        grid=(steps,),
        in_specs=[
            pl.BlockSpec((vectors // steps, rows), lambda i: (i, 0)),
            WHOLE,
            WHOLE,
            pl.BlockSpec((chips // steps, held, more), lambda i: (i, 0, 0)),
        ],
        out_specs=pl.BlockSpec((chips // steps, held, both + more), lambda i: (i, 0, 0)),
        compiler_params=params(),
        name="project",
    )(zt, high, low, overlap)


def add_up(parts):
    def kernel(in_ref, out_ref):
        out_ref[...] = jnp.broadcast_to(jnp.sum(in_ref[...], axis=0, keepdims=True), out_ref.shape)

    return pl.pallas_call(
        kernel,
        out_shape=f32(*parts.shape),
        in_specs=[WHOLE],
        out_specs=WHOLE,
        compiler_params=params(),
        name="add_up",
    )(parts)


def solve(total, factor_first, factor_second):
    chips, held, more = total.shape
    width = factor_first.shape[0]
    cut = width // 2
    full = lax.Precision.HIGHEST
    rows = (((1,), (1,)), ((), ()))

    def kernel(total_ref, first_ref, second_ref, out_ref):
        pieces = total_ref[:, :, 2 * width :].reshape(2, width, cut)
        overlap = jnp.concatenate([pieces[0], pieces[1]], axis=1)
        first = total_ref[:, :, :width].reshape(chips * held, width)
        second = total_ref[:, :, width : 2 * width].reshape(chips * held, width)
        first = lax.dot_general(first, first_ref[...], rows, precision=full)
        second = second - jnp.dot(first, overlap, precision=full)
        out_ref[:, :width] = first
        out_ref[:, width:] = lax.dot_general(second, second_ref[...], rows, precision=full)

    return pl.pallas_call(
        kernel,
        out_shape=f32(chips * held, 2 * width),
        in_specs=[WHOLE] * 3,
        out_specs=WHOLE,
        compiler_params=params(),
        name="solve",
    )(total, factor_first, factor_second)


def update(where, zt, weights, high, low, flip, order, places):
    vectors, rows = zt.shape
    block = vectors // (HALVES * places)
    count = len(order)

    def target(w, j):
        return (w[0] ^ flip) * places + partner(w[2], j, w[0], w[1])

    def kernel(where_ref, *refs):
        z_refs, (weights_ref, high_ref, low_ref), outs = refs[:count], refs[count:-count], refs[-count:]
        rows = [weights_ref[times(target(where_ref, j), block)] for j in order]
        change = dot3(in_two(jnp.concatenate(rows, axis=0)), (high_ref[...], low_ref[...]), 0)
        for i in range(count):
            outs[i][...] = z_refs[i][...] - change[i * block : (i + 1) * block]

    def z_spec(j):
        return pl.BlockSpec((block, rows), lambda i, w: (target(w, j), 0))

    return pl.pallas_call(
        kernel,
        out_shape=[f32(block, rows)] * count,
        grid_spec=pltpu.PrefetchScalarGridSpec(
            num_scalar_prefetch=1,
            grid=(1,),
            in_specs=[z_spec(j) for j in order] + [WHOLE] * 3,
            out_specs=[pl.BlockSpec((block, rows), lambda i, w: (0, 0))] * count,
        ),
        compiler_params=params(),
        name="update",
    )(where, *[zt] * count, weights, high, low)


def gather(where, pieces, names, places, out=None):
    block, part = pieces[0].shape
    n = len(pieces)

    def kernel(where_ref, *refs):
        ins, dst, sems = refs[:n], refs[-2], refs[-1]
        copies = []
        for i, (flip, j) in enumerate(names):
            core = where_ref[1] ^ flip
            target = dst.at[times(core, block), times(partner(where_ref[2], j, where_ref[0], core), part)]
            copies.append(pltpu.make_async_copy(ins[i], target, sems.at[i]))
        copy_all(copies)

    held = [] if out is None else [out]
    return pl.pallas_call(
        kernel,
        out_shape=f32(CORES * block, places * part),
        in_specs=[SCALAR] + [ANY] * (n + len(held)),
        out_specs=ANY,
        scratch_shapes=[pltpu.SemaphoreType.DMA((n,))],
        input_output_aliases={n + 1: 0} if held else {},
        compiler_params=params(),
        name="gather",
    )(where, *pieces, *held)


def body(vectors_in, panel_first, panel_second, factor_first, factor_second):
    blocks, places = lax.axis_size("block"), lax.axis_size("place")
    chips = blocks * HALVES * places
    held = vectors_in.shape[0]
    where = jnp.stack([lax.axis_index(name) for name in INNER]).astype(jnp.int32)

    def permute(piece, target):
        index = [(c, h, p) for c in range(CORES) for h in range(HALVES) for p in range(places)]
        return lax.ppermute(piece, INNER, [(i, index.index(target(*at))) for i, at in enumerate(index)])

    order = (3, 1, 0, 2)
    pieces = pack_panels(where, panel_first.T, panel_second.T, order[:2], places)
    pieces += pack_panels(where, panel_first.T, panel_second.T, order[2:], places)
    own = [permute(piece, lambda c, h, p: (h, c, partner(p, j, c, h))) for j, piece in zip(order, pieces)]
    other = [lax.ppermute(piece, "core", [(0, 1), (1, 0)]) for piece in own]
    vectors_in, own, other = lax.optimization_barrier((vectors_in, own, other))
    zt = lax.all_to_all(vectors_in, CHIPS, split_axis=1, concat_axis=0, tiled=True)
    zt = zt.reshape(chips * held, -1)
    zt, own, other = lax.optimization_barrier((zt, own, other))
    high, low, overlap = prepare(where, own, other, order, chips, held)

    partial = project(zt, high, low, overlap)
    parts = lax.all_to_all(partial, CHIPS, split_axis=0, concat_axis=0, tiled=True)
    total = lax.all_to_all(add_up(parts), CHIPS, split_axis=0, concat_axis=0, tiled=True)
    weights = solve(total, factor_first, factor_second)

    pieces, names = [], []
    for flip in range(HALVES):
        for some in (order[:2], order[2:]):
            for j, piece in zip(some, update(where, zt, weights, high, low, flip, some, places)):
                pieces.append(permute(piece, lambda c, h, p: (h, c ^ flip, partner(p, j, c, h))))
                names.append((flip, j))
    out = None
    for some in (slice(0, 4), slice(4, 7), slice(7, 8)):
        out = gather(where, pieces[some], names[some], places, out)
    return out


def solution(mesh):
    rows, cols = mesh.devices.shape
    blocks, places = rows // CORES, cols // HALVES
    split = Mesh(mesh.devices.reshape(blocks, CORES, HALVES, places), ("block",) + INNER)
    row, col = ("block", "core"), ("half", "place")
    return jax.shard_map(
        body,
        mesh=split,
        in_specs=(P(row + col, None), P(row, col), P(row, col), P(), P()),
        out_specs=P(col, row),
        check_vma=False,
    )
```

time: 295 us -> 282 us (0.956)
  blocking collectives: 59.4 us -> 139 us
  waiting for transfers between devices: 161 us -> 93.1 us
  Pallas kernels: 40.8 us -> 27.5 us
  starting transfers between devices: 24.5 us -> 18.6 us
    all_to_all x1 -> x2, blocking collectives: 24.8 us -> 110 us  [the longest x1 85.1 us: body(): lax.all_to_all(vectors_in, CHIPS, split_axis=1, concat_axis=0, tiled=True)]
    all_to_all x1 -> x0, waiting for transfers between devices: 62.4 us -> none  [body(): lax.all_to_all(vectors_in, CHIPS, split_axis=1, concat_axis=0, tiled=True)]
    all_to_all x1 -> x0, starting transfers between devices: 9.31 us -> none  [body(): lax.all_to_all(vectors_in, CHIPS, split_axis=1, concat_axis=0, tiled=True)]
    pallas_call x4 -> x8, Pallas kernels: 19.7 us -> 11.4 us  [the longest x4 7.77 us: update(): pl.pallas_call(kernel, out_shape=[f32(block, rows)] * count, grid_spec=pl...]
    all_to_all x1, blocking collectives: 34.6 us -> 28.8 us  [body(): lax.all_to_all(partial, CHIPS, split_axis=0, concat_axis=0, tiled=True)]
    pallas_call x1, Pallas kernels: 8.52 us -> 5.32 us  [project(): pl.pallas_call(kernel, out_shape=f32(chips, held, both + more), grid=(ste...]
    pallas_call x1, Pallas kernels: 8.16 us -> 5.12 us  [prepare(): pl.pallas_call(kernel, out_shape=[bf16, bf16, f32(chips, held, count)], g...]
  transfers between devices with their start and end apart: 14 -> 16, of which waited for: 6 -> 8; matrix products, arithmetic and copies ran while one was open for 0% -> 0% of each run, Pallas kernels for 7% -> 4%
where the time goes in v3:
time: 282 us; the launch traced here: 281 us
  blocking collectives  139 us (49%)
  waiting for transfers between devices  93.1 us (33%)
  Pallas kernels  27.5 us (10%)
  starting transfers between devices  18.6 us (7%)
  local copies, waits for them, and re-layouts  2.83 us (1%)
    ppermute x12, waiting for transfers between devices, permute(): lax.ppermute(piece, INNER, [(i, index.index(target(*at))) for i, at in en...  89.5 us
    all_to_all x1, blocking collectives, body(): lax.all_to_all(vectors_in, CHIPS, split_axis=1, concat_axis=0, tiled=True)  85.1 us
    all_to_all x1, blocking collectives, body(): lax.all_to_all(partial, CHIPS, split_axis=0, concat_axis=0, tiled=True)  28.8 us
    all_to_all x1, blocking collectives, body(): lax.all_to_all(add_up(parts), CHIPS, split_axis=0, concat_axis=0, tiled=T...  25 us
    ppermute x12, starting transfers between devices, permute(): lax.ppermute(piece, INNER, [(i, index.index(target(*at))) for i, at in en...  18 us
    pallas_call x4, Pallas kernels, update(): pl.pallas_call(kernel, out_shape=[f32(block, rows)] * count, grid_spec=pl...  7.77 us
    pallas_call x3, Pallas kernels, gather(): pl.pallas_call(kernel, out_shape=f32(CORES * block, places * part), in_sp...  5.65 us
  transfers between devices with their start and end apart: 16, of which 8 were waited for; matrix products, arithmetic and copies ran while one was open for 0% of the time, Pallas kernels for 4%

profile of v3, /device:TPU:0, one launch (start us, length us, event | category | flops | bytes accessed | tf_op | source)
XLA Modules:
  0.0 281.3 jit_solution(16089397968363343499)
XLA Ops:
  0.1 1.4 copy-done
  1.5 1.4 copy-done.1
  3.5 4.2 %collective-permute-start = (f32[64,3072]{1,0:T(8,128)S(1)}, f32[64,3072]{1,0:T(8,128)S(1)}, u32[]{:S(2)}, u32[]{:S(2)}) collective-permute-start(f32[64,3072]{1,0:T(8,128)S(1)} %get-tuple-element.38), channel_id=1, source_target_pairs={{0,3},{1,2},{2,1},{3,0},{4,9},{5,8},{6,11},{7,10},{8,5},{9,4},{10,... | collective-permute-start | bytes 2359304 | tf_op jit(solution)/shard_map/ppermute | solution.py:269
  9.3 1.5 collective-permute-start.3
  10.8 31.8 %collective-permute-done.refs_0_ = f32[64,3072]{1,0:T(8,128)S(1)} collective-permute-done((f32[64,3072]{1,0:T(8,128)S(1)}, f32[64,3072]{1,0:T(8,128)S(1)}, u32[]{:S(2)}, u32[]{:S(2)}) %collective-permute-start) | collective-permute-done | bytes 786464 | tf_op jit(solution)/shard_map/ppermute | solution.py:269
  43.1 1.4 collective-permute-done.3.refs_3_
  44.8 1.1 collective-permute-done.5.refs_5_
  48.2 85.1 %all_to_all.29 = f32[8,64,3072]{2,0,1:T(8,128)S(1)} all-to-all(f32[8,64,3072]{2,0,1:T(8,128)S(1)} %bitcast.26), channel_id=1, replica_groups=mesh['block'=8,'core'=2,'half'=2,'place'=4] {'block','half','place'}, dimensions={1} | all-to-all | bytes 12582912 | tf_op jit(solution)/shard_map/all_to_all | solution.py:277
  133.3 5.1 %prepare.1 = (bf16[512,3072]{1,0:T(8,128)(2,1)S(1)}, bf16[512,3072]{1,0:T(8,128)(2,1)S(1)}, f32[64,8,128]{2,1,0:T(8,128)S(1)}) custom-call(s32[3]{0:T(128)S(1)} %pad_add_fusion.where_ref, f32[64,3072]{1,0:T(8,128)S(1)} %collective-permute-done.refs_0_, f32[64,3072]{1,0:T(8,128)S(1)} %collective-permute-done.1.refs_1_, ...), custom_call_target="tpu_custom_call" | custom-call | tf_op jit(solution)/shard_map/prepare/pallas_call | solution.py:120
  138.4 5.3 %project.1 = f32[64,8,640]{2,1,0:T(8,128)S(1)} custom-call(f32[512,3072]{1,0:T(8,128)S(1)} %bitcast.9, bf16[512,3072]{1,0:T(8,128)(2,1)S(1)} %get-tuple-element.60.high_ref.refs_3_, bf16[512,3072]{1,0:T(8,128)(2,1)S(1)} %get-tuple-element.61.low_ref.refs_4_, f32[64,8,128]{2,1,0:T(8,128)S(1)} %get-tuple-element.62.overlap_ref), custom_call_target="tpu_custom_call" | custom-call | tf_op jit(solution)/shard_map/project/pallas_call | solution.py:146
  143.7 28.8 %all_to_all.30.in_ref = f32[64,8,640]{2,1,0:T(8,128)S(1)} all-to-all(f32[64,8,640]{2,1,0:T(8,128)S(1)} %project.1), channel_id=1, replica_groups=mesh['block'=8,'core'=2,'half'=2,'place'=4] {'block','half','place'}, dimensions={0} | all-to-all | bytes 2621440 | tf_op jit(solution)/shard_map/all_to_all | solution.py:283
  172.7 25.0 %all_to_all.31.total_ref = f32[64,8,640]{2,1,0:T(8,128)S(1)} all-to-all(f32[64,8,640]{2,1,0:T(8,128)S(1)} %add_up.1), channel_id=1, replica_groups=mesh['block'=8,'core'=2,'half'=2,'place'=4] {'block','half','place'}, dimensions={0} | all-to-all | bytes 2621440 | tf_op jit(solution)/shard_map/all_to_all | solution.py:284
  197.7 2.2 solve.1.refs_2_
  199.9 1.9 update.6
  203.2 1.9 update.7
  205.9 1.9 update.4
  207.8 1.9 update.5
  209.8 5.3 %collective-permute-start.9 = (f32[64,3072]{1,0:T(8,128)S(1)}, f32[64,3072]{1,0:T(8,128)S(1)}, u32[]{:S(2)}, u32[]{:S(2)}) collective-permute-start(f32[64,3072]{1,0:T(8,128)S(1)} %get-tuple-element.64), channel_id=1, source_target_pairs={{0,7},{1,6},{2,5},{3,4},{4,13},{5,12},{6,15},{7,14},{8,1},{9,0},{1... | collective-permute-start | bytes 2359304 | tf_op jit(solution)/shard_map/ppermute | solution.py:269
  215.1 28.0 %collective-permute-done.12.refs_0_ = f32[64,3072]{1,0:T(8,128)S(1)} collective-permute-done((f32[64,3072]{1,0:T(8,128)S(1)}, f32[64,3072]{1,0:T(8,128)S(1)}, u32[]{:S(2)}, u32[]{:S(2)}) %collective-permute-start.12) | collective-permute-done | bytes 786464 | tf_op jit(solution)/shard_map/ppermute | solution.py:269
  243.2 4.0 %collective-permute-start.8 = (f32[64,3072]{1,0:T(8,128)S(1)}, f32[64,3072]{1,0:T(8,128)S(1)}, u32[]{:S(2)}, u32[]{:S(2)}) collective-permute-start(f32[64,3072]{1,0:T(8,128)S(1)} %get-tuple-element.63), channel_id=1, source_target_pairs={{0,6},{1,7},{2,4},{3,5},{4,12},{5,13},{6,14},{7,15},{8,0},{9,1},{1... | collective-permute-start | bytes 2359304 | tf_op jit(solution)/shard_map/ppermute | solution.py:269
  247.2 28.2 %collective-permute-done.15.refs_3_ = f32[64,3072]{1,0:T(8,128)S(1)} collective-permute-done((f32[64,3072]{1,0:T(8,128)S(1)}, f32[64,3072]{1,0:T(8,128)S(1)}, u32[]{:S(2)}, u32[]{:S(2)}) %collective-permute-start.15) | collective-permute-done | bytes 786464 | tf_op jit(solution)/shard_map/ppermute | solution.py:269
  275.4 2.2 gather.3.refs_3_
  277.7 2.0 gather.4.refs_1_
  279.7 1.4 gather.5
  (35 shorter events, 7.6 us)
Async XLA Ops:
  0.1 1.4 copy-start
  1.5 1.4 copy-start.1
  3.5 39.0 %collective-permute-start = (f32[64,3072]{1,0:T(8,128)S(1)}, f32[64,3072]{1,0:T(8,128)S(1)}, u32[]{:S(2)}, u32[]{:S(2)}) collective-permute-start(f32[64,3072]{1,0:T(8,128)S(1)} %get-tuple-element.38), channel_id=1, source_target_pairs={{0,3},{1,2},{2,1},{3,0},{4,9},{5,8},{6,11},{7,10},{8,5},{9,4},{10,... | collective-permute-start | bytes 2359304 | tf_op jit(solution)/shard_map/ppermute | solution.py:269
  7.8 40.5 %copy-start.4 = (f32[8,196608]{1,0:T(8,128)S(1)}, f32[8,196608]{1,0:T(8,128)}, u32[]{:S(2)}) copy-start(f32[8,196608]{1,0:T(8,128)} %param.5) | copy-start | bytes 18874372
  7.8 34.8 %collective-permute-start.1 = (f32[64,3072]{1,0:T(8,128)S(1)}, f32[64,3072]{1,0:T(8,128)S(1)}, u32[]{:S(2)}, u32[]{:S(2)}) collective-permute-start(f32[64,3072]{1,0:T(8,128)S(1)} %get-tuple-element.39), channel_id=1, source_target_pairs={{0,1},{1,0},{2,3},{3,2},{4,11},{5,10},{6,9},{7,8},{8,7},{9,6},{10,... | collective-permute-start | bytes 2359304 | tf_op jit(solution)/shard_map/ppermute | solution.py:269
  8.4 34.6 %collective-permute-start.2 = (f32[64,3072]{1,0:T(8,128)S(1)}, f32[64,3072]{1,0:T(8,128)S(1)}, u32[]{:S(2)}, u32[]{:S(2)}) collective-permute-start(f32[64,3072]{1,0:T(8,128)S(1)} %get-tuple-element.40), channel_id=1, source_target_pairs={{0,0},{1,1},{2,2},{3,3},{4,10},{5,11},{6,8},{7,9},{8,6},{9,7},{10,... | collective-permute-start | bytes 2359304 | tf_op jit(solution)/shard_map/ppermute | solution.py:269
  9.3 35.3 %collective-permute-start.3 = (f32[64,3072]{1,0:T(8,128)S(1)}, f32[64,3072]{1,0:T(8,128)S(1)}, u32[]{:S(2)}, u32[]{:S(2)}) collective-permute-start(f32[64,3072]{1,0:T(8,128)S(1)} %get-tuple-element.41), channel_id=1, source_target_pairs={{0,2},{1,3},{2,0},{3,1},{4,8},{5,9},{6,10},{7,11},{8,4},{9,5},{10,... | collective-permute-start | bytes 2359304 | tf_op jit(solution)/shard_map/ppermute | solution.py:269
  42.5 2.3 collective-permute-start.4
  42.5 3.4 %collective-permute-start.5 = (f32[64,3072]{1,0:T(8,128)S(1)}, f32[64,3072]{1,0:T(8,128)S(1)}, u32[]{:S(2)}, u32[]{:S(2)}) collective-permute-start(f32[64,3072]{1,0:T(8,128)S(1)} %collective-permute-done.1.refs_1_), channel_id=1, source_target_pairs={{0,8},{8,0},{1,9},{9,1},{2,10},{10,2},{3,11},{11,3},{4,12},{12,4},... | collective-permute-start | bytes 2359304 | tf_op jit(solution)/shard_map/ppermute | solution.py:275
  43.1 4.0 %collective-permute-start.6 = (f32[64,3072]{1,0:T(8,128)S(1)}, f32[64,3072]{1,0:T(8,128)S(1)}, u32[]{:S(2)}, u32[]{:S(2)}) collective-permute-start(f32[64,3072]{1,0:T(8,128)S(1)} %collective-permute-done.2.refs_2_), channel_id=1, source_target_pairs={{0,8},{8,0},{1,9},{9,1},{2,10},{10,2},{3,11},{11,3},{4,12},{12,4},... | collective-permute-start | bytes 2359304 | tf_op jit(solution)/shard_map/ppermute | solution.py:275
  44.6 3.6 %collective-permute-start.7 = (f32[64,3072]{1,0:T(8,128)S(1)}, f32[64,3072]{1,0:T(8,128)S(1)}, u32[]{:S(2)}, u32[]{:S(2)}) collective-permute-start(f32[64,3072]{1,0:T(8,128)S(1)} %collective-permute-done.3.refs_3_), channel_id=1, source_target_pairs={{0,8},{8,0},{1,9},{9,1},{2,10},{10,2},{3,11},{11,3},{4,12},{12,4},... | collective-permute-start | bytes 2359304 | tf_op jit(solution)/shard_map/ppermute | solution.py:275
  172.6 25.1 %copy-start.2 = (f32[256,256]{1,0:T(8,128)S(1)}, f32[256,256]{1,0:T(8,128)}, u32[]{:S(2)}) copy-start(f32[256,256]{1,0:T(8,128)} %first_ref.1) | copy-start | bytes 786436
  172.6 25.1 %copy-start.3 = (f32[256,256]{1,0:T(8,128)S(1)}, f32[256,256]{1,0:T(8,128)}, u32[]{:S(2)}) copy-start(f32[256,256]{1,0:T(8,128)} %second_ref.1) | copy-start | bytes 786436
  201.9 41.3 %collective-permute-start.12 = (f32[64,3072]{1,0:T(8,128)S(1)}, f32[64,3072]{1,0:T(8,128)S(1)}, u32[]{:S(2)}, u32[]{:S(2)}) collective-permute-start(f32[64,3072]{1,0:T(8,128)S(1)} %get-tuple-element.67), channel_id=1, source_target_pairs={{0,3},{1,2},{2,1},{3,0},{4,9},{5,8},{6,11},{7,10},{8,5},{9,4},{10,... | collective-permute-start | bytes 2359304 | tf_op jit(solution)/shard_map/ppermute | solution.py:269
  202.8 40.4 %collective-permute-start.13 = (f32[64,3072]{1,0:T(8,128)S(1)}, f32[64,3072]{1,0:T(8,128)S(1)}, u32[]{:S(2)}, u32[]{:S(2)}) collective-permute-start(f32[64,3072]{1,0:T(8,128)S(1)} %get-tuple-element.68), channel_id=1, source_target_pairs={{0,1},{1,0},{2,3},{3,2},{4,11},{5,10},{6,9},{7,8},{8,7},{9,6},{10,... | collective-permute-start | bytes 2359304 | tf_op jit(solution)/shard_map/ppermute | solution.py:269
  205.2 38.0 %collective-permute-start.14 = (f32[64,3072]{1,0:T(8,128)S(1)}, f32[64,3072]{1,0:T(8,128)S(1)}, u32[]{:S(2)}, u32[]{:S(2)}) collective-permute-start(f32[64,3072]{1,0:T(8,128)S(1)} %get-tuple-element.69), channel_id=1, source_target_pairs={{0,0},{1,1},{2,2},{3,3},{4,10},{5,11},{6,8},{7,9},{8,6},{9,7},{10,... | collective-permute-start | bytes 2359304 | tf_op jit(solution)/shard_map/ppermute | solution.py:269
  209.8 67.9 %collective-permute-start.9 = (f32[64,3072]{1,0:T(8,128)S(1)}, f32[64,3072]{1,0:T(8,128)S(1)}, u32[]{:S(2)}, u32[]{:S(2)}) collective-permute-start(f32[64,3072]{1,0:T(8,128)S(1)} %get-tuple-element.64), channel_id=1, source_target_pairs={{0,7},{1,6},{2,5},{3,4},{4,13},{5,12},{6,15},{7,14},{8,1},{9,0},{1... | collective-permute-start | bytes 2359304 | tf_op jit(solution)/shard_map/ppermute | solution.py:269
  215.1 62.6 %collective-permute-start.10 = (f32[64,3072]{1,0:T(8,128)S(1)}, f32[64,3072]{1,0:T(8,128)S(1)}, u32[]{:S(2)}, u32[]{:S(2)}) collective-permute-start(f32[64,3072]{1,0:T(8,128)S(1)} %get-tuple-element.65), channel_id=1, source_target_pairs={{0,5},{1,4},{2,7},{3,6},{4,15},{5,14},{6,13},{7,12},{8,3},{9,2},{1... | collective-permute-start | bytes 2359304 | tf_op jit(solution)/shard_map/ppermute | solution.py:269
  243.2 32.3 %collective-permute-start.15 = (f32[64,3072]{1,0:T(8,128)S(1)}, f32[64,3072]{1,0:T(8,128)S(1)}, u32[]{:S(2)}, u32[]{:S(2)}) collective-permute-start(f32[64,3072]{1,0:T(8,128)S(1)} %get-tuple-element.70), channel_id=1, source_target_pairs={{0,2},{1,3},{2,0},{3,1},{4,8},{5,9},{6,10},{7,11},{8,4},{9,5},{10,... | collective-permute-start | bytes 2359304 | tf_op jit(solution)/shard_map/ppermute | solution.py:269
  243.2 34.5 %collective-permute-start.11 = (f32[64,3072]{1,0:T(8,128)S(1)}, f32[64,3072]{1,0:T(8,128)S(1)}, u32[]{:S(2)}, u32[]{:S(2)}) collective-permute-start(f32[64,3072]{1,0:T(8,128)S(1)} %get-tuple-element.66), channel_id=1, source_target_pairs={{0,4},{1,5},{2,6},{3,7},{4,14},{5,15},{6,12},{7,13},{8,2},{9,3},{1... | collective-permute-start | bytes 2359304 | tf_op jit(solution)/shard_map/ppermute | solution.py:269
  243.2 36.5 %collective-permute-start.8 = (f32[64,3072]{1,0:T(8,128)S(1)}, f32[64,3072]{1,0:T(8,128)S(1)}, u32[]{:S(2)}, u32[]{:S(2)}) collective-permute-start(f32[64,3072]{1,0:T(8,128)S(1)} %get-tuple-element.63), channel_id=1, source_target_pairs={{0,6},{1,7},{2,4},{3,5},{4,12},{5,13},{6,14},{7,15},{8,0},{9,1},{1... | collective-permute-start | bytes 2359304 | tf_op jit(solution)/shard_map/ppermute | solution.py:269

commit v4 on v3

--- a/solution.py
+++ b/solution.py
@@ -86,7 +86,7 @@
     held_cols, rows = own[0].shape[0] // 2, own[0].shape[1]
     count = places * held_cols
     width = CORES * count
-    steps = 6
+    steps = 2
     tile = rows // steps
 
     def kernel(where_ref, *refs):
@@ -173,45 +173,37 @@
     )(parts)
 
 
-def solve(total, factor_first, factor_second):
-    chips, held, more = total.shape
-    width = factor_first.shape[0]
+def update(where, zt, total, factors, high, low, flip, order, places):
+    vectors, rows = zt.shape
+    chips, held, _ = total.shape
+    block = vectors // (HALVES * places)
+    width = high.shape[0] // 2
     cut = width // 2
+    count = len(order)
     full = lax.Precision.HIGHEST
-    rows = (((1,), (1,)), ((), ()))
-
-    def kernel(total_ref, first_ref, second_ref, out_ref):
+    across = (((1,), (1,)), ((), ()))
+
+    def target(w, j):
+        return (w[0] ^ flip) * places + partner(w[2], j, w[0], w[1])
+
+    def kernel(where_ref, *refs):
+        z_refs, (total_ref, first_ref, second_ref, high_ref, low_ref), outs = (
+            refs[:count],
+            refs[count:-count],
+            refs[-count:],
+        )
+        sums = [total_ref[times(target(where_ref, j), block // held)] for j in order]
+        first, second = (
+            jnp.concatenate([v[:, :, at].reshape(block, width) for v in sums], axis=0)
+            for at in (slice(0, width), slice(width, 2 * width))
+        )
         pieces = total_ref[:, :, 2 * width :].reshape(2, width, cut)
         overlap = jnp.concatenate([pieces[0], pieces[1]], axis=1)
-        first = total_ref[:, :, :width].reshape(chips * held, width)
-        second = total_ref[:, :, width : 2 * width].reshape(chips * held, width)
-        first = lax.dot_general(first, first_ref[...], rows, precision=full)
+        first = lax.dot_general(first, first_ref[...], across, precision=full)
         second = second - jnp.dot(first, overlap, precision=full)
-        out_ref[:, :width] = first
-        out_ref[:, width:] = lax.dot_general(second, second_ref[...], rows, precision=full)
-
-    return pl.pallas_call(
-        kernel,
-        out_shape=f32(chips * held, 2 * width),
-        in_specs=[WHOLE] * 3,
-        out_specs=WHOLE,
-        compiler_params=params(),
-        name="solve",
-    )(total, factor_first, factor_second)
-
-
-def update(where, zt, weights, high, low, flip, order, places):
-    vectors, rows = zt.shape
-    block = vectors // (HALVES * places)
-    count = len(order)
-
-    def target(w, j):
-        return (w[0] ^ flip) * places + partner(w[2], j, w[0], w[1])
-
-    def kernel(where_ref, *refs):
-        z_refs, (weights_ref, high_ref, low_ref), outs = refs[:count], refs[count:-count], refs[-count:]
-        rows = [weights_ref[times(target(where_ref, j), block)] for j in order]
-        change = dot3(in_two(jnp.concatenate(rows, axis=0)), (high_ref[...], low_ref[...]), 0)
+        second = lax.dot_general(second, second_ref[...], across, precision=full)
+        weights = jnp.concatenate([first, second], axis=1)
+        change = dot3(in_two(weights), (high_ref[...], low_ref[...]), 0)
         for i in range(count):
             outs[i][...] = z_refs[i][...] - change[i * block : (i + 1) * block]
 
@@ -224,12 +216,12 @@
         grid_spec=pltpu.PrefetchScalarGridSpec(
             num_scalar_prefetch=1,
             grid=(1,),
-            in_specs=[z_spec(j) for j in order] + [WHOLE] * 3,
+            in_specs=[z_spec(j) for j in order] + [WHOLE] * 5,
             out_specs=[pl.BlockSpec((block, rows), lambda i, w: (0, 0))] * count,
         ),
         compiler_params=params(),
         name="update",
-    )(where, *[zt] * count, weights, high, low)
+    )(where, *[zt] * count, total, *factors, high, low)
 
 
 def gather(where, pieces, names, places, out=None):
@@ -282,17 +274,18 @@
     partial = project(zt, high, low, overlap)
     parts = lax.all_to_all(partial, CHIPS, split_axis=0, concat_axis=0, tiled=True)
     total = lax.all_to_all(add_up(parts), CHIPS, split_axis=0, concat_axis=0, tiled=True)
-    weights = solve(total, factor_first, factor_second)
+    factors = factor_first, factor_second
 
     pieces, names = [], []
     for flip in range(HALVES):
         for some in (order[:2], order[2:]):
-            for j, piece in zip(some, update(where, zt, weights, high, low, flip, some, places)):
+            for j, piece in zip(some, update(where, zt, total, factors, high, low, flip, some, places)):
                 pieces.append(permute(piece, lambda c, h, p: (h, c ^ flip, partner(p, j, c, h))))
                 names.append((flip, j))
+    last = (3, 6, 7)
     out = None
-    for some in (slice(0, 4), slice(4, 7), slice(7, 8)):
-        out = gather(where, pieces[some], names[some], places, out)
+    for some in ([i for i in range(len(pieces)) if i not in last], last):
+        out = gather(where, [pieces[i] for i in some], [names[i] for i in some], places, out)
     return out
 
 

time: 282 us -> 281 us (level)
  waiting for transfers between devices: 93.1 us -> 88.9 us
    pallas_call x4, Pallas kernels: 7.77 us -> 13.8 us  [update(): pl.pallas_call(kernel, out_shape=[f32(block, rows)] * count, grid_spec=pl...]
    ppermute x12, waiting for transfers between devices: 89.5 us -> 85.3 us  [permute(): lax.ppermute(piece, INNER, [(i, index.index(target(*at))) for i, at in en...]
    pallas_call x3 -> x2, Pallas kernels: 5.65 us -> 4.48 us  [gather(): pl.pallas_call(kernel, out_shape=f32(CORES * block, places * part), in_sp...]
  transfers between devices with their start and end apart: 16 -> 16, of which waited for: 8 -> 9; matrix products, arithmetic and copies ran while one was open for 0% -> 0% of each run, Pallas kernels for 4% -> 5%
where the time goes in v4:
time: 281 us
  blocking collectives  139 us (49%)
  waiting for transfers between devices  88.9 us (32%)
  Pallas kernels  29.3 us (10%)
  starting transfers between devices  20.3 us (7%)
  local copies, waits for them, and re-layouts  2.83 us (1%)
    ppermute x12, waiting for transfers between devices, permute(): lax.ppermute(piece, INNER, [(i, index.index(target(*at))) for i, at in en...  85.3 us
    all_to_all x1, blocking collectives, body(): lax.all_to_all(vectors_in, CHIPS, split_axis=1, concat_axis=0, tiled=True)  85.1 us
    all_to_all x1, blocking collectives, body(): lax.all_to_all(partial, CHIPS, split_axis=0, concat_axis=0, tiled=True)  28.8 us
    all_to_all x1, blocking collectives, body(): lax.all_to_all(add_up(parts), CHIPS, split_axis=0, concat_axis=0, tiled=T...  25 us
    ppermute x12, starting transfers between devices, permute(): lax.ppermute(piece, INNER, [(i, index.index(target(*at))) for i, at in en...  19.7 us
    pallas_call x4, Pallas kernels, update(): pl.pallas_call(kernel, out_shape=[f32(block, rows)] * count, grid_spec=pl...  13.8 us
  transfers between devices with their start and end apart: 16, of which 9 were waited for; matrix products, arithmetic and copies ran while one was open for 0% of the time, Pallas kernels for 5%

profile of v4, /device:TPU:0, one launch (start us, length us, event | category | flops | bytes accessed | tf_op | source)
XLA Modules:
  0.0 280.6 jit_solution(6867158593663533830)
XLA Ops:
  0.1 1.4 copy-done
  1.5 1.4 copy-done.1
  3.5 4.2 %collective-permute-start = (f32[64,3072]{1,0:T(8,128)S(1)}, f32[64,3072]{1,0:T(8,128)S(1)}, u32[]{:S(2)}, u32[]{:S(2)}) collective-permute-start(f32[64,3072]{1,0:T(8,128)S(1)} %get-tuple-element.38), channel_id=1, source_target_pairs={{0,3},{1,2},{2,1},{3,0},{4,9},{5,8},{6,11},{7,10},{8,5},{9,4},{10,... | collective-permute-start | bytes 2359304 | tf_op jit(solution)/shard_map/ppermute | solution.py:261
  9.3 1.5 collective-permute-start.3
  10.8 31.8 %collective-permute-done.refs_0_ = f32[64,3072]{1,0:T(8,128)S(1)} collective-permute-done((f32[64,3072]{1,0:T(8,128)S(1)}, f32[64,3072]{1,0:T(8,128)S(1)}, u32[]{:S(2)}, u32[]{:S(2)}) %collective-permute-start) | collective-permute-done | bytes 786464 | tf_op jit(solution)/shard_map/ppermute | solution.py:261
  43.1 1.4 collective-permute-done.3.refs_3_
  48.2 85.1 %all_to_all.29 = f32[8,64,3072]{2,0,1:T(8,128)S(1)} all-to-all(f32[8,64,3072]{2,0,1:T(8,128)S(1)} %bitcast.26), channel_id=1, replica_groups=mesh['block'=8,'core'=2,'half'=2,'place'=4] {'block','half','place'}, dimensions={1} | all-to-all | bytes 12582912 | tf_op jit(solution)/shard_map/all_to_all | solution.py:269
  133.3 4.3 %prepare.1 = (bf16[512,3072]{1,0:T(8,128)(2,1)S(1)}, bf16[512,3072]{1,0:T(8,128)(2,1)S(1)}, f32[64,8,128]{2,1,0:T(8,128)S(1)}) custom-call(s32[3]{0:T(128)S(1)} %pad_add_fusion.where_ref, f32[64,3072]{1,0:T(8,128)S(1)} %collective-permute-done.refs_0_, f32[64,3072]{1,0:T(8,128)S(1)} %collective-permute-done.1.refs_1_, ...), custom_call_target="tpu_custom_call" | custom-call | tf_op jit(solution)/shard_map/prepare/pallas_call | solution.py:120
  137.5 5.3 %project.1 = f32[64,8,640]{2,1,0:T(8,128)S(1)} custom-call(f32[512,3072]{1,0:T(8,128)S(1)} %bitcast.9, bf16[512,3072]{1,0:T(8,128)(2,1)S(1)} %get-tuple-element.60.high_ref.refs_5_, bf16[512,3072]{1,0:T(8,128)(2,1)S(1)} %get-tuple-element.61.low_ref.refs_6_, f32[64,8,128]{2,1,0:T(8,128)S(1)} %get-tuple-element.62.overlap_ref), custom_call_target="tpu_custom_call" | custom-call | tf_op jit(solution)/shard_map/project/pallas_call | solution.py:146
  142.9 28.8 %all_to_all.30.in_ref = f32[64,8,640]{2,1,0:T(8,128)S(1)} all-to-all(f32[64,8,640]{2,1,0:T(8,128)S(1)} %project.1), channel_id=1, replica_groups=mesh['block'=8,'core'=2,'half'=2,'place'=4] {'block','half','place'}, dimensions={0} | all-to-all | bytes 2621440 | tf_op jit(solution)/shard_map/all_to_all | solution.py:275
  171.9 25.0 %all_to_all.31.refs_2_ = f32[64,8,640]{2,1,0:T(8,128)S(1)} all-to-all(f32[64,8,640]{2,1,0:T(8,128)S(1)} %add_up.1), channel_id=1, replica_groups=mesh['block'=8,'core'=2,'half'=2,'place'=4] {'block','half','place'}, dimensions={0} | all-to-all | bytes 2621440 | tf_op jit(solution)/shard_map/all_to_all | solution.py:276
  196.8 3.4 %update.6 = (f32[64,3072]{1,0:T(8,128)S(1)}, f32[64,3072]{1,0:T(8,128)S(1)}) custom-call(s32[3]{0:T(128)S(1)} %pad_add_fusion.where_ref, f32[512,3072]{1,0:T(8,128)S(1)} %bitcast.10, f32[512,3072]{1,0:T(8,128)S(1)} %bitcast.11, f32[64,8,640]{2,1,0:T(8,128)S(1)} %all_to_all.31.refs_2_, f32[256,256]{1,0:T(8,128)S(1)} %copy-done.2, f32[256,256]{1,0:T(8,128)S(1)} %copy-done.3, ...), custom_call_target="tpu_custom_call" | custom-call | tf_op jit(solution)/shard_map/update/pallas_call | solution.py:213
  200.3 1.1 collective-permute-start.11
  201.8 3.4 %update.4 = (f32[64,3072]{1,0:T(8,128)S(1)}, f32[64,3072]{1,0:T(8,128)S(1)}) custom-call(s32[3]{0:T(128)S(1)} %pad_add_fusion.where_ref, f32[512,3072]{1,0:T(8,128)S(1)} %bitcast.12, f32[512,3072]{1,0:T(8,128)S(1)} %bitcast.13, f32[64,8,640]{2,1,0:T(8,128)S(1)} %all_to_all.31.refs_2_, f32[256,256]{1,0:T(8,128)S(1)} %copy-done.2, f32[256,256]{1,0:T(8,128)S(1)} %copy-done.3, ...), custom_call_target="tpu_custom_call" | custom-call | tf_op jit(solution)/shard_map/update/pallas_call | solution.py:213
  206.0 3.5 %collective-permute-start.8 = (f32[64,3072]{1,0:T(8,128)S(1)}, f32[64,3072]{1,0:T(8,128)S(1)}, u32[]{:S(2)}, u32[]{:S(2)}) collective-permute-start(f32[64,3072]{1,0:T(8,128)S(1)} %get-tuple-element.63), channel_id=1, source_target_pairs={{0,2},{1,3},{2,0},{3,1},{4,8},{5,9},{6,10},{7,11},{8,4},{9,5},{10,... | collective-permute-start | bytes 2359304 | tf_op jit(solution)/shard_map/ppermute | solution.py:261
  209.5 3.4 %update.7 = (f32[64,3072]{1,0:T(8,128)S(1)}, f32[64,3072]{1,0:T(8,128)S(1)}) custom-call(s32[3]{0:T(128)S(1)} %pad_add_fusion.where_ref, f32[512,3072]{1,0:T(8,128)S(1)} %bitcast.14, f32[512,3072]{1,0:T(8,128)S(1)} %bitcast.15, f32[64,8,640]{2,1,0:T(8,128)S(1)} %all_to_all.31.refs_2_, f32[256,256]{1,0:T(8,128)S(1)} %copy-done.2, f32[256,256]{1,0:T(8,128)S(1)} %copy-done.3, ...), custom_call_target="tpu_custom_call" | custom-call | tf_op jit(solution)/shard_map/update/pallas_call | solution.py:213
  212.9 2.7 collective-permute-start.14
  215.7 3.4 %update.5 = (f32[64,3072]{1,0:T(8,128)S(1)}, f32[64,3072]{1,0:T(8,128)S(1)}) custom-call(s32[3]{0:T(128)S(1)} %pad_add_fusion.where_ref, f32[512,3072]{1,0:T(8,128)S(1)} %bitcast.16, f32[512,3072]{1,0:T(8,128)S(1)} %bitcast.17, f32[64,8,640]{2,1,0:T(8,128)S(1)} %all_to_all.31.refs_2_, f32[256,256]{1,0:T(8,128)S(1)} %copy-done.2, f32[256,256]{1,0:T(8,128)S(1)} %copy-done.3, ...), custom_call_target="tpu_custom_call" | custom-call | tf_op jit(solution)/shard_map/update/pallas_call | solution.py:213
  219.1 21.3 %collective-permute-done.11.refs_0_ = f32[64,3072]{1,0:T(8,128)S(1)} collective-permute-done((f32[64,3072]{1,0:T(8,128)S(1)}, f32[64,3072]{1,0:T(8,128)S(1)}, u32[]{:S(2)}, u32[]{:S(2)}) %collective-permute-start.11) | collective-permute-done | bytes 786464 | tf_op jit(solution)/shard_map/ppermute | solution.py:261
  240.5 4.6 %collective-permute-start.10 = (f32[64,3072]{1,0:T(8,128)S(1)}, f32[64,3072]{1,0:T(8,128)S(1)}, u32[]{:S(2)}, u32[]{:S(2)}) collective-permute-start(f32[64,3072]{1,0:T(8,128)S(1)} %get-tuple-element.65), channel_id=1, source_target_pairs={{0,6},{1,7},{2,4},{3,5},{4,12},{5,13},{6,14},{7,15},{8,0},{9,1},{1... | collective-permute-start | bytes 2359304 | tf_op jit(solution)/shard_map/ppermute | solution.py:261
  245.1 7.9 %collective-permute-done.14.refs_3_ = f32[64,3072]{1,0:T(8,128)S(1)} collective-permute-done((f32[64,3072]{1,0:T(8,128)S(1)}, f32[64,3072]{1,0:T(8,128)S(1)}, u32[]{:S(2)}, u32[]{:S(2)}) %collective-permute-start.14) | collective-permute-done | bytes 786464 | tf_op jit(solution)/shard_map/ppermute | solution.py:261
  252.9 22.9 %collective-permute-done.15.refs_4_ = f32[64,3072]{1,0:T(8,128)S(1)} collective-permute-done((f32[64,3072]{1,0:T(8,128)S(1)}, f32[64,3072]{1,0:T(8,128)S(1)}, u32[]{:S(2)}, u32[]{:S(2)}) %collective-permute-start.15) | collective-permute-done | bytes 786464 | tf_op jit(solution)/shard_map/ppermute | solution.py:261
  275.9 2.5 gather.2.refs_3_
  278.4 2.0 gather.3
  (33 shorter events, 7.8 us)
Async XLA Ops:
  0.1 1.4 copy-start
  1.5 1.4 copy-start.1
  3.5 39.0 %collective-permute-start = (f32[64,3072]{1,0:T(8,128)S(1)}, f32[64,3072]{1,0:T(8,128)S(1)}, u32[]{:S(2)}, u32[]{:S(2)}) collective-permute-start(f32[64,3072]{1,0:T(8,128)S(1)} %get-tuple-element.38), channel_id=1, source_target_pairs={{0,3},{1,2},{2,1},{3,0},{4,9},{5,8},{6,11},{7,10},{8,5},{9,4},{10,... | collective-permute-start | bytes 2359304 | tf_op jit(solution)/shard_map/ppermute | solution.py:261
  7.8 40.5 %copy-start.4 = (f32[8,196608]{1,0:T(8,128)S(1)}, f32[8,196608]{1,0:T(8,128)}, u32[]{:S(2)}) copy-start(f32[8,196608]{1,0:T(8,128)} %param.5) | copy-start | bytes 18874372
  7.8 34.8 %collective-permute-start.1 = (f32[64,3072]{1,0:T(8,128)S(1)}, f32[64,3072]{1,0:T(8,128)S(1)}, u32[]{:S(2)}, u32[]{:S(2)}) collective-permute-start(f32[64,3072]{1,0:T(8,128)S(1)} %get-tuple-element.39), channel_id=1, source_target_pairs={{0,1},{1,0},{2,3},{3,2},{4,11},{5,10},{6,9},{7,8},{8,7},{9,6},{10,... | collective-permute-start | bytes 2359304 | tf_op jit(solution)/shard_map/ppermute | solution.py:261
  8.4 34.6 %collective-permute-start.2 = (f32[64,3072]{1,0:T(8,128)S(1)}, f32[64,3072]{1,0:T(8,128)S(1)}, u32[]{:S(2)}, u32[]{:S(2)}) collective-permute-start(f32[64,3072]{1,0:T(8,128)S(1)} %get-tuple-element.40), channel_id=1, source_target_pairs={{0,0},{1,1},{2,2},{3,3},{4,10},{5,11},{6,8},{7,9},{8,6},{9,7},{10,... | collective-permute-start | bytes 2359304 | tf_op jit(solution)/shard_map/ppermute | solution.py:261
  9.3 35.3 %collective-permute-start.3 = (f32[64,3072]{1,0:T(8,128)S(1)}, f32[64,3072]{1,0:T(8,128)S(1)}, u32[]{:S(2)}, u32[]{:S(2)}) collective-permute-start(f32[64,3072]{1,0:T(8,128)S(1)} %get-tuple-element.41), channel_id=1, source_target_pairs={{0,2},{1,3},{2,0},{3,1},{4,8},{5,9},{6,10},{7,11},{8,4},{9,5},{10,... | collective-permute-start | bytes 2359304 | tf_op jit(solution)/shard_map/ppermute | solution.py:261
  42.5 2.3 collective-permute-start.4
  42.5 3.4 %collective-permute-start.5 = (f32[64,3072]{1,0:T(8,128)S(1)}, f32[64,3072]{1,0:T(8,128)S(1)}, u32[]{:S(2)}, u32[]{:S(2)}) collective-permute-start(f32[64,3072]{1,0:T(8,128)S(1)} %collective-permute-done.1.refs_1_), channel_id=1, source_target_pairs={{0,8},{8,0},{1,9},{9,1},{2,10},{10,2},{3,11},{11,3},{4,12},{12,4},... | collective-permute-start | bytes 2359304 | tf_op jit(solution)/shard_map/ppermute | solution.py:267
  43.1 4.0 %collective-permute-start.6 = (f32[64,3072]{1,0:T(8,128)S(1)}, f32[64,3072]{1,0:T(8,128)S(1)}, u32[]{:S(2)}, u32[]{:S(2)}) collective-permute-start(f32[64,3072]{1,0:T(8,128)S(1)} %collective-permute-done.2.refs_2_), channel_id=1, source_target_pairs={{0,8},{8,0},{1,9},{9,1},{2,10},{10,2},{3,11},{11,3},{4,12},{12,4},... | collective-permute-start | bytes 2359304 | tf_op jit(solution)/shard_map/ppermute | solution.py:267
  44.6 3.6 %collective-permute-start.7 = (f32[64,3072]{1,0:T(8,128)S(1)}, f32[64,3072]{1,0:T(8,128)S(1)}, u32[]{:S(2)}, u32[]{:S(2)}) collective-permute-start(f32[64,3072]{1,0:T(8,128)S(1)} %collective-permute-done.3.refs_3_), channel_id=1, source_target_pairs={{0,8},{8,0},{1,9},{9,1},{2,10},{10,2},{3,11},{11,3},{4,12},{12,4},... | collective-permute-start | bytes 2359304 | tf_op jit(solution)/shard_map/ppermute | solution.py:267
  171.7 25.1 %copy-start.2 = (f32[256,256]{1,0:T(8,128)S(1)}, f32[256,256]{1,0:T(8,128)}, u32[]{:S(2)}) copy-start(f32[256,256]{1,0:T(8,128)} %refs_3_.7) | copy-start | bytes 786436
  171.7 25.1 %copy-start.3 = (f32[256,256]{1,0:T(8,128)S(1)}, f32[256,256]{1,0:T(8,128)}, u32[]{:S(2)}) copy-start(f32[256,256]{1,0:T(8,128)} %refs_4_.7) | copy-start | bytes 786436
  200.3 40.2 %collective-permute-start.11 = (f32[64,3072]{1,0:T(8,128)S(1)}, f32[64,3072]{1,0:T(8,128)S(1)}, u32[]{:S(2)}, u32[]{:S(2)}) collective-permute-start(f32[64,3072]{1,0:T(8,128)S(1)} %get-tuple-element.66), channel_id=1, source_target_pairs={{0,3},{1,2},{2,1},{3,0},{4,9},{5,8},{6,11},{7,10},{8,5},{9,4},{10,... | collective-permute-start | bytes 2359304 | tf_op jit(solution)/shard_map/ppermute | solution.py:261
  201.4 39.0 %collective-permute-start.12 = (f32[64,3072]{1,0:T(8,128)S(1)}, f32[64,3072]{1,0:T(8,128)S(1)}, u32[]{:S(2)}, u32[]{:S(2)}) collective-permute-start(f32[64,3072]{1,0:T(8,128)S(1)} %get-tuple-element.67), channel_id=1, source_target_pairs={{0,1},{1,0},{2,3},{3,2},{4,11},{5,10},{6,9},{7,8},{8,7},{9,6},{10,... | collective-permute-start | bytes 2359304 | tf_op jit(solution)/shard_map/ppermute | solution.py:261
  205.3 35.2 %collective-permute-start.13 = (f32[64,3072]{1,0:T(8,128)S(1)}, f32[64,3072]{1,0:T(8,128)S(1)}, u32[]{:S(2)}, u32[]{:S(2)}) collective-permute-start(f32[64,3072]{1,0:T(8,128)S(1)} %get-tuple-element.68), channel_id=1, source_target_pairs={{0,0},{1,1},{2,2},{3,3},{4,10},{5,11},{6,8},{7,9},{8,6},{9,7},{10,... | collective-permute-start | bytes 2359304 | tf_op jit(solution)/shard_map/ppermute | solution.py:261
  206.0 72.4 %collective-permute-start.8 = (f32[64,3072]{1,0:T(8,128)S(1)}, f32[64,3072]{1,0:T(8,128)S(1)}, u32[]{:S(2)}, u32[]{:S(2)}) collective-permute-start(f32[64,3072]{1,0:T(8,128)S(1)} %get-tuple-element.63), channel_id=1, source_target_pairs={{0,2},{1,3},{2,0},{3,1},{4,8},{5,9},{6,10},{7,11},{8,4},{9,5},{10,... | collective-permute-start | bytes 2359304 | tf_op jit(solution)/shard_map/ppermute | solution.py:261
  212.9 40.0 %collective-permute-start.14 = (f32[64,3072]{1,0:T(8,128)S(1)}, f32[64,3072]{1,0:T(8,128)S(1)}, u32[]{:S(2)}, u32[]{:S(2)}) collective-permute-start(f32[64,3072]{1,0:T(8,128)S(1)} %get-tuple-element.69), channel_id=1, source_target_pairs={{0,7},{1,6},{2,5},{3,4},{4,13},{5,12},{6,15},{7,14},{8,1},{9,0},{1... | collective-permute-start | bytes 2359304 | tf_op jit(solution)/shard_map/ppermute | solution.py:261
  240.4 35.4 %collective-permute-start.15 = (f32[64,3072]{1,0:T(8,128)S(1)}, f32[64,3072]{1,0:T(8,128)S(1)}, u32[]{:S(2)}, u32[]{:S(2)}) collective-permute-start(f32[64,3072]{1,0:T(8,128)S(1)} %get-tuple-element.70), channel_id=1, source_target_pairs={{0,5},{1,4},{2,7},{3,6},{4,15},{5,14},{6,13},{7,12},{8,3},{9,2},{1... | collective-permute-start | bytes 2359304 | tf_op jit(solution)/shard_map/ppermute | solution.py:261
  240.4 38.0 %collective-permute-start.9 = (f32[64,3072]{1,0:T(8,128)S(1)}, f32[64,3072]{1,0:T(8,128)S(1)}, u32[]{:S(2)}, u32[]{:S(2)}) collective-permute-start(f32[64,3072]{1,0:T(8,128)S(1)} %get-tuple-element.64), channel_id=1, source_target_pairs={{0,4},{1,5},{2,6},{3,7},{4,14},{5,15},{6,12},{7,13},{8,2},{9,3},{1... | collective-permute-start | bytes 2359304 | tf_op jit(solution)/shard_map/ppermute | solution.py:261
  240.5 38.0 %collective-permute-start.10 = (f32[64,3072]{1,0:T(8,128)S(1)}, f32[64,3072]{1,0:T(8,128)S(1)}, u32[]{:S(2)}, u32[]{:S(2)}) collective-permute-start(f32[64,3072]{1,0:T(8,128)S(1)} %get-tuple-element.65), channel_id=1, source_target_pairs={{0,6},{1,7},{2,4},{3,5},{4,12},{5,13},{6,14},{7,15},{8,0},{9,1},{1... | collective-permute-start | bytes 2359304 | tf_op jit(solution)/shard_map/ppermute | solution.py:261

commit v5 on v4

--- a/solution.py
+++ b/solution.py
@@ -5,7 +5,7 @@
 from jax.experimental.pallas import tpu as pltpu
 from jax.sharding import Mesh, PartitionSpec as P
 
-CHIPS = ("block", "half", "place")
+CHIPS = ("half", "place", "block")
 INNER = ("core", "half", "place")
 CORES = 2
 HALVES = 2
@@ -175,8 +175,9 @@
 
 def update(where, zt, total, factors, high, low, flip, order, places):
     vectors, rows = zt.shape
-    chips, held, _ = total.shape
-    block = vectors // (HALVES * places)
+    cols, blocks, held, _ = total.shape
+    block = cols * held
+    zt = zt.reshape(cols, blocks, held, rows)
     width = high.shape[0] // 2
     cut = width // 2
     count = len(order)
@@ -192,12 +193,12 @@
             refs[count:-count],
             refs[-count:],
         )
-        sums = [total_ref[times(target(where_ref, j), block // held)] for j in order]
+        sums = [total_ref[:, pl.ds(target(where_ref, j), 1)] for j in order]
         first, second = (
-            jnp.concatenate([v[:, :, at].reshape(block, width) for v in sums], axis=0)
+            jnp.concatenate([v[:, :, :, at].reshape(block, width) for v in sums], axis=0)
             for at in (slice(0, width), slice(width, 2 * width))
         )
-        pieces = total_ref[:, :, 2 * width :].reshape(2, width, cut)
+        pieces = total_ref[:, :, :, 2 * width :].reshape(2, width, cut)
         overlap = jnp.concatenate([pieces[0], pieces[1]], axis=1)
         first = lax.dot_general(first, first_ref[...], across, precision=full)
         second = second - jnp.dot(first, overlap, precision=full)
@@ -205,10 +206,10 @@
         weights = jnp.concatenate([first, second], axis=1)
         change = dot3(in_two(weights), (high_ref[...], low_ref[...]), 0)
         for i in range(count):
-            outs[i][...] = z_refs[i][...] - change[i * block : (i + 1) * block]
+            outs[i][...] = z_refs[i][...].reshape(block, rows) - change[i * block : (i + 1) * block]
 
     def z_spec(j):
-        return pl.BlockSpec((block, rows), lambda i, w: (target(w, j), 0))
+        return pl.BlockSpec((cols, 1, held, rows), lambda i, w: (0, target(w, j), 0, 0))
 
     return pl.pallas_call(
         kernel,
@@ -265,8 +266,9 @@
     pieces += pack_panels(where, panel_first.T, panel_second.T, order[2:], places)
     own = [permute(piece, lambda c, h, p: (h, c, partner(p, j, c, h))) for j, piece in zip(order, pieces)]
     other = [lax.ppermute(piece, "core", [(0, 1), (1, 0)]) for piece in own]
-    vectors_in, own, other = lax.optimization_barrier((vectors_in, own, other))
-    zt = lax.all_to_all(vectors_in, CHIPS, split_axis=1, concat_axis=0, tiled=True)
+    zt = vectors_in.reshape(held, blocks, chips // blocks, -1).transpose(2, 1, 0, 3)
+    zt, own, other = lax.optimization_barrier((zt.reshape(chips, held, -1), own, other))
+    zt = lax.all_to_all(zt, CHIPS, split_axis=0, concat_axis=0, tiled=True)
     zt = zt.reshape(chips * held, -1)
     zt, own, other = lax.optimization_barrier((zt, own, other))
     high, low, overlap = prepare(where, own, other, order, chips, held)
@@ -274,6 +276,7 @@
     partial = project(zt, high, low, overlap)
     parts = lax.all_to_all(partial, CHIPS, split_axis=0, concat_axis=0, tiled=True)
     total = lax.all_to_all(add_up(parts), CHIPS, split_axis=0, concat_axis=0, tiled=True)
+    total = total.reshape(chips // blocks, blocks, held, -1)
     factors = factor_first, factor_second
 
     pieces, names = [], []

time: 281 us -> 277 us (0.986)
  starting transfers between devices: 20.3 us -> 16.9 us
  blocking collectives: 139 us -> 136 us
    ppermute x12, starting transfers between devices: 19.7 us -> 16.3 us  [permute(): lax.ppermute(piece, INNER, [(i, index.index(target(*at))) for i, at in en...]
    ppermute x12, waiting for transfers between devices: 85.3 us -> 88.5 us  [permute(): lax.ppermute(piece, INNER, [(i, index.index(target(*at))) for i, at in en...]
  transfers between devices with their start and end apart: 16 -> 16, of which waited for: 9 -> 8; matrix products, arithmetic and copies ran while one was open for 0% -> 0% of each run, Pallas kernels for 5% -> 5%
where the time goes in v5:
time: 277 us
  blocking collectives  136 us (49%)
  waiting for transfers between devices  91.4 us (33%)
  Pallas kernels  29.3 us (11%)
  starting transfers between devices  16.9 us (6%)
  local copies, waits for them, and re-layouts  3.56 us (1%)
    ppermute x12, waiting for transfers between devices, permute(): lax.ppermute(piece, INNER, [(i, index.index(target(*at))) for i, at in en...  88.5 us
    all_to_all x1, blocking collectives, body(): zt = lax.all_to_all(zt, CHIPS, split_axis=0, concat_axis=0, tiled=True)  84.9 us
    all_to_all x1, blocking collectives, body(): lax.all_to_all(partial, CHIPS, split_axis=0, concat_axis=0, tiled=True)  26.1 us
    all_to_all x1, blocking collectives, body(): lax.all_to_all(add_up(parts), CHIPS, split_axis=0, concat_axis=0, tiled=T...  24.5 us
    ppermute x12, starting transfers between devices, permute(): lax.ppermute(piece, INNER, [(i, index.index(target(*at))) for i, at in en...  16.3 us
    pallas_call x4, Pallas kernels, update(): pl.pallas_call(kernel, out_shape=[f32(block, rows)] * count, grid_spec=pl...  13.8 us
  transfers between devices with their start and end apart: 16, of which 8 were waited for; matrix products, arithmetic and copies ran while one was open for 0% of the time, Pallas kernels for 5%

profile of v5, /device:TPU:0, one launch (start us, length us, event | category | flops | bytes accessed | tf_op | source)
XLA Modules:
  0.0 277.1 jit_solution(4233113350523480439)
XLA Ops:
  0.1 1.4 copy-done
  1.5 1.4 copy-done.1
  3.5 4.2 %collective-permute-start = (f32[64,3072]{1,0:T(8,128)S(1)}, f32[64,3072]{1,0:T(8,128)S(1)}, u32[]{:S(2)}, u32[]{:S(2)}) collective-permute-start(f32[64,3072]{1,0:T(8,128)S(1)} %get-tuple-element.38), channel_id=1, source_target_pairs={{0,3},{1,2},{2,1},{3,0},{4,9},{5,8},{6,11},{7,10},{8,5},{9,4},{10,... | collective-permute-start | bytes 2359304 | tf_op jit(solution)/shard_map/ppermute | solution.py:262
  9.3 1.5 collective-permute-start.3
  10.8 31.8 %collective-permute-done.refs_0_ = f32[64,3072]{1,0:T(8,128)S(1)} collective-permute-done((f32[64,3072]{1,0:T(8,128)S(1)}, f32[64,3072]{1,0:T(8,128)S(1)}, u32[]{:S(2)}, u32[]{:S(2)}) %collective-permute-start) | collective-permute-done | bytes 786464 | tf_op jit(solution)/shard_map/ppermute | solution.py:262
  43.1 1.4 collective-permute-done.3.refs_3_
  45.9 1.1 collective-permute-done.6.refs_6_
  48.2 84.9 %all_to_all.15 = f32[64,8,3072]{2,1,0:T(8,128)S(1)} all-to-all(f32[64,8,3072]{2,1,0:T(8,128)S(1)} %bitcast.33), channel_id=1, replica_groups=mesh['block'=8,'core'=2,'half'=2,'place'=4] {'half','place','block'}, dimensions={0} | all-to-all | bytes 12582912 | tf_op jit(solution)/shard_map/all_to_all | solution.py:271
  133.1 4.3 %prepare.1 = (bf16[512,3072]{1,0:T(8,128)(2,1)S(1)}, bf16[512,3072]{1,0:T(8,128)(2,1)S(1)}, f32[64,8,128]{2,1,0:T(8,128)S(1)}) custom-call(s32[3]{0:T(128)S(1)} %pad_add_fusion.where_ref, f32[64,3072]{1,0:T(8,128)S(1)} %collective-permute-done.refs_0_, f32[64,3072]{1,0:T(8,128)S(1)} %collective-permute-done.1.refs_1_, ...), custom_call_target="tpu_custom_call" | custom-call | tf_op jit(solution)/shard_map/prepare/pallas_call | solution.py:120
  137.4 5.3 %project.1 = f32[64,8,640]{2,1,0:T(8,128)S(1)} custom-call(f32[512,3072]{1,0:T(8,128)S(1)} %bitcast.12, bf16[512,3072]{1,0:T(8,128)(2,1)S(1)} %get-tuple-element.60.high_ref.refs_5_, bf16[512,3072]{1,0:T(8,128)(2,1)S(1)} %get-tuple-element.61.low_ref.refs_6_, f32[64,8,128]{2,1,0:T(8,128)S(1)} %get-tuple-element.62.overlap_ref), custom_call_target="tpu_custom_call" | custom-call | tf_op jit(solution)/shard_map/project/pallas_call | solution.py:146
  142.7 26.1 %all_to_all.16.in_ref = f32[64,8,640]{2,1,0:T(8,128)S(1)} all-to-all(f32[64,8,640]{2,1,0:T(8,128)S(1)} %project.1), channel_id=1, replica_groups=mesh['block'=8,'core'=2,'half'=2,'place'=4] {'half','place','block'}, dimensions={0} | all-to-all | bytes 2621440 | tf_op jit(solution)/shard_map/all_to_all | solution.py:277
  169.0 24.5 %all_to_all.17 = f32[64,8,640]{2,1,0:T(8,128)S(1)} all-to-all(f32[64,8,640]{2,1,0:T(8,128)S(1)} %add_up.1), channel_id=1, replica_groups=mesh['block'=8,'core'=2,'half'=2,'place'=4] {'half','place','block'}, dimensions={0} | all-to-all | bytes 2621440 | tf_op jit(solution)/shard_map/all_to_all | solution.py:278
  193.5 3.4 %update.6 = (f32[64,3072]{1,0:T(8,128)S(1)}, f32[64,3072]{1,0:T(8,128)S(1)}) custom-call(s32[3]{0:T(128)S(1)} %pad_add_fusion.where_ref, f32[8,8,8,3072]{3,2,1,0:T(8,128)S(1)} %bitcast.13, f32[8,8,8,3072]{3,2,1,0:T(8,128)S(1)} %bitcast.14, f32[8,8,8,640]{3,2,1,0:T(8,128)S(1)} %bitcast.21, f32[256,256]{1,0:T(8,128)S(1)} %copy-done.2, ...), custom_call_target="tpu_custom_call" | custom-call | tf_op jit(solution)/shard_map/update/pallas_call | solution.py:214
  197.0 1.2 collective-permute-start.11
  198.8 3.4 %update.4 = (f32[64,3072]{1,0:T(8,128)S(1)}, f32[64,3072]{1,0:T(8,128)S(1)}) custom-call(s32[3]{0:T(128)S(1)} %pad_add_fusion.where_ref, f32[8,8,8,3072]{3,2,1,0:T(8,128)S(1)} %bitcast.15, f32[8,8,8,3072]{3,2,1,0:T(8,128)S(1)} %bitcast.16, f32[8,8,8,640]{3,2,1,0:T(8,128)S(1)} %bitcast.22, f32[256,256]{1,0:T(8,128)S(1)} %copy-done.2, ...), custom_call_target="tpu_custom_call" | custom-call | tf_op jit(solution)/shard_map/update/pallas_call | solution.py:214
  203.0 3.4 %update.5 = (f32[64,3072]{1,0:T(8,128)S(1)}, f32[64,3072]{1,0:T(8,128)S(1)}) custom-call(s32[3]{0:T(128)S(1)} %pad_add_fusion.where_ref, f32[8,8,8,3072]{3,2,1,0:T(8,128)S(1)} %bitcast.17, f32[8,8,8,3072]{3,2,1,0:T(8,128)S(1)} %bitcast.18, f32[8,8,8,640]{3,2,1,0:T(8,128)S(1)} %bitcast.23, f32[256,256]{1,0:T(8,128)S(1)} %copy-done.2, ...), custom_call_target="tpu_custom_call" | custom-call | tf_op jit(solution)/shard_map/update/pallas_call | solution.py:214
  206.4 3.4 %update.7 = (f32[64,3072]{1,0:T(8,128)S(1)}, f32[64,3072]{1,0:T(8,128)S(1)}) custom-call(s32[3]{0:T(128)S(1)} %pad_add_fusion.where_ref, f32[8,8,8,3072]{3,2,1,0:T(8,128)S(1)} %bitcast.19, f32[8,8,8,3072]{3,2,1,0:T(8,128)S(1)} %bitcast.20, f32[8,8,8,640]{3,2,1,0:T(8,128)S(1)} %bitcast.24, f32[256,256]{1,0:T(8,128)S(1)} %copy-done.2, ...), custom_call_target="tpu_custom_call" | custom-call | tf_op jit(solution)/shard_map/update/pallas_call | solution.py:214
  209.9 3.0 %collective-permute-start.8 = (f32[64,3072]{1,0:T(8,128)S(1)}, f32[64,3072]{1,0:T(8,128)S(1)}, u32[]{:S(2)}, u32[]{:S(2)}) collective-permute-start(f32[64,3072]{1,0:T(8,128)S(1)} %get-tuple-element.63), channel_id=1, source_target_pairs={{0,2},{1,3},{2,0},{3,1},{4,8},{5,9},{6,10},{7,11},{8,4},{9,5},{10,... | collective-permute-start | bytes 2359304 | tf_op jit(solution)/shard_map/ppermute | solution.py:262
  212.9 3.4 %collective-permute-start.14 = (f32[64,3072]{1,0:T(8,128)S(1)}, f32[64,3072]{1,0:T(8,128)S(1)}, u32[]{:S(2)}, u32[]{:S(2)}) collective-permute-start(f32[64,3072]{1,0:T(8,128)S(1)} %get-tuple-element.69), channel_id=1, source_target_pairs={{0,7},{1,6},{2,5},{3,4},{4,13},{5,12},{6,15},{7,14},{8,1},{9,0},{1... | collective-permute-start | bytes 2359304 | tf_op jit(solution)/shard_map/ppermute | solution.py:262
  216.3 23.1 %collective-permute-done.11.refs_0_ = f32[64,3072]{1,0:T(8,128)S(1)} collective-permute-done((f32[64,3072]{1,0:T(8,128)S(1)}, f32[64,3072]{1,0:T(8,128)S(1)}, u32[]{:S(2)}, u32[]{:S(2)}) %collective-permute-start.11) | collective-permute-done | bytes 786464 | tf_op jit(solution)/shard_map/ppermute | solution.py:262
  240.2 15.1 %collective-permute-done.14.refs_3_ = f32[64,3072]{1,0:T(8,128)S(1)} collective-permute-done((f32[64,3072]{1,0:T(8,128)S(1)}, f32[64,3072]{1,0:T(8,128)S(1)}, u32[]{:S(2)}, u32[]{:S(2)}) %collective-permute-start.14) | collective-permute-done | bytes 786464 | tf_op jit(solution)/shard_map/ppermute | solution.py:262
  255.3 17.1 %collective-permute-done.15.refs_4_ = f32[64,3072]{1,0:T(8,128)S(1)} collective-permute-done((f32[64,3072]{1,0:T(8,128)S(1)}, f32[64,3072]{1,0:T(8,128)S(1)}, u32[]{:S(2)}, u32[]{:S(2)}) %collective-permute-start.15) | collective-permute-done | bytes 786464 | tf_op jit(solution)/shard_map/ppermute | solution.py:262
  272.4 2.5 gather.2.refs_3_
  274.9 2.0 gather.3
  (34 shorter events, 7.6 us)
Async XLA Ops:
  0.1 1.4 copy-start
  1.5 1.4 copy-start.1
  3.5 39.0 %collective-permute-start = (f32[64,3072]{1,0:T(8,128)S(1)}, f32[64,3072]{1,0:T(8,128)S(1)}, u32[]{:S(2)}, u32[]{:S(2)}) collective-permute-start(f32[64,3072]{1,0:T(8,128)S(1)} %get-tuple-element.38), channel_id=1, source_target_pairs={{0,3},{1,2},{2,1},{3,0},{4,9},{5,8},{6,11},{7,10},{8,5},{9,4},{10,... | collective-permute-start | bytes 2359304 | tf_op jit(solution)/shard_map/ppermute | solution.py:262
  7.8 36.8 %copy-start.4 = (f32[8,196608]{1,0:T(8,128)S(1)}, f32[8,196608]{1,0:T(8,128)}, u32[]{:S(2)}) copy-start(f32[8,196608]{1,0:T(8,128)} %param.5) | copy-start | bytes 18874372
  7.8 34.8 %collective-permute-start.1 = (f32[64,3072]{1,0:T(8,128)S(1)}, f32[64,3072]{1,0:T(8,128)S(1)}, u32[]{:S(2)}, u32[]{:S(2)}) collective-permute-start(f32[64,3072]{1,0:T(8,128)S(1)} %get-tuple-element.39), channel_id=1, source_target_pairs={{0,1},{1,0},{2,3},{3,2},{4,11},{5,10},{6,9},{7,8},{8,7},{9,6},{10,... | collective-permute-start | bytes 2359304 | tf_op jit(solution)/shard_map/ppermute | solution.py:262
  8.4 34.6 %collective-permute-start.2 = (f32[64,3072]{1,0:T(8,128)S(1)}, f32[64,3072]{1,0:T(8,128)S(1)}, u32[]{:S(2)}, u32[]{:S(2)}) collective-permute-start(f32[64,3072]{1,0:T(8,128)S(1)} %get-tuple-element.40), channel_id=1, source_target_pairs={{0,0},{1,1},{2,2},{3,3},{4,10},{5,11},{6,8},{7,9},{8,6},{9,7},{10,... | collective-permute-start | bytes 2359304 | tf_op jit(solution)/shard_map/ppermute | solution.py:262
  9.3 35.3 %collective-permute-start.3 = (f32[64,3072]{1,0:T(8,128)S(1)}, f32[64,3072]{1,0:T(8,128)S(1)}, u32[]{:S(2)}, u32[]{:S(2)}) collective-permute-start(f32[64,3072]{1,0:T(8,128)S(1)} %get-tuple-element.41), channel_id=1, source_target_pairs={{0,2},{1,3},{2,0},{3,1},{4,8},{5,9},{6,10},{7,11},{8,4},{9,5},{10,... | collective-permute-start | bytes 2359304 | tf_op jit(solution)/shard_map/ppermute | solution.py:262
  42.5 2.8 %collective-permute-start.4 = (f32[64,3072]{1,0:T(8,128)S(1)}, f32[64,3072]{1,0:T(8,128)S(1)}, u32[]{:S(2)}, u32[]{:S(2)}) collective-permute-start(f32[64,3072]{1,0:T(8,128)S(1)} %collective-permute-done.refs_0_), channel_id=1, source_target_pairs={{0,8},{8,0},{1,9},{9,1},{2,10},{10,2},{3,11},{11,3},{4,12},{12,4},... | collective-permute-start | bytes 2359304 | tf_op jit(solution)/shard_map/ppermute | solution.py:268
  42.5 3.4 %collective-permute-start.5 = (f32[64,3072]{1,0:T(8,128)S(1)}, f32[64,3072]{1,0:T(8,128)S(1)}, u32[]{:S(2)}, u32[]{:S(2)}) collective-permute-start(f32[64,3072]{1,0:T(8,128)S(1)} %collective-permute-done.1.refs_1_), channel_id=1, source_target_pairs={{0,8},{8,0},{1,9},{9,1},{2,10},{10,2},{3,11},{11,3},{4,12},{12,4},... | collective-permute-start | bytes 2359304 | tf_op jit(solution)/shard_map/ppermute | solution.py:268
  43.1 4.0 %collective-permute-start.6 = (f32[64,3072]{1,0:T(8,128)S(1)}, f32[64,3072]{1,0:T(8,128)S(1)}, u32[]{:S(2)}, u32[]{:S(2)}) collective-permute-start(f32[64,3072]{1,0:T(8,128)S(1)} %collective-permute-done.2.refs_2_), channel_id=1, source_target_pairs={{0,8},{8,0},{1,9},{9,1},{2,10},{10,2},{3,11},{11,3},{4,12},{12,4},... | collective-permute-start | bytes 2359304 | tf_op jit(solution)/shard_map/ppermute | solution.py:268
  44.6 3.6 %collective-permute-start.7 = (f32[64,3072]{1,0:T(8,128)S(1)}, f32[64,3072]{1,0:T(8,128)S(1)}, u32[]{:S(2)}, u32[]{:S(2)}) collective-permute-start(f32[64,3072]{1,0:T(8,128)S(1)} %collective-permute-done.3.refs_3_), channel_id=1, source_target_pairs={{0,8},{8,0},{1,9},{9,1},{2,10},{10,2},{3,11},{11,3},{4,12},{12,4},... | collective-permute-start | bytes 2359304 | tf_op jit(solution)/shard_map/ppermute | solution.py:268
  168.8 24.7 %copy-start.2 = (f32[256,256]{1,0:T(8,128)S(1)}, f32[256,256]{1,0:T(8,128)}, u32[]{:S(2)}) copy-start(f32[256,256]{1,0:T(8,128)} %refs_3_.7) | copy-start | bytes 786436
  168.8 24.7 %copy-start.3 = (f32[256,256]{1,0:T(8,128)S(1)}, f32[256,256]{1,0:T(8,128)}, u32[]{:S(2)}) copy-start(f32[256,256]{1,0:T(8,128)} %refs_4_.7) | copy-start | bytes 786436
  197.0 42.5 %collective-permute-start.11 = (f32[64,3072]{1,0:T(8,128)S(1)}, f32[64,3072]{1,0:T(8,128)S(1)}, u32[]{:S(2)}, u32[]{:S(2)}) collective-permute-start(f32[64,3072]{1,0:T(8,128)S(1)} %get-tuple-element.66), channel_id=1, source_target_pairs={{0,3},{1,2},{2,1},{3,0},{4,9},{5,8},{6,11},{7,10},{8,5},{9,4},{10,... | collective-permute-start | bytes 2359304 | tf_op jit(solution)/shard_map/ppermute | solution.py:262
  198.2 41.3 %collective-permute-start.12 = (f32[64,3072]{1,0:T(8,128)S(1)}, f32[64,3072]{1,0:T(8,128)S(1)}, u32[]{:S(2)}, u32[]{:S(2)}) collective-permute-start(f32[64,3072]{1,0:T(8,128)S(1)} %get-tuple-element.67), channel_id=1, source_target_pairs={{0,1},{1,0},{2,3},{3,2},{4,11},{5,10},{6,9},{7,8},{8,7},{9,6},{10,... | collective-permute-start | bytes 2359304 | tf_op jit(solution)/shard_map/ppermute | solution.py:262
  202.3 37.2 %collective-permute-start.13 = (f32[64,3072]{1,0:T(8,128)S(1)}, f32[64,3072]{1,0:T(8,128)S(1)}, u32[]{:S(2)}, u32[]{:S(2)}) collective-permute-start(f32[64,3072]{1,0:T(8,128)S(1)} %get-tuple-element.68), channel_id=1, source_target_pairs={{0,0},{1,1},{2,2},{3,3},{4,10},{5,11},{6,8},{7,9},{8,6},{9,7},{10,... | collective-permute-start | bytes 2359304 | tf_op jit(solution)/shard_map/ppermute | solution.py:262
  209.9 65.0 %collective-permute-start.8 = (f32[64,3072]{1,0:T(8,128)S(1)}, f32[64,3072]{1,0:T(8,128)S(1)}, u32[]{:S(2)}, u32[]{:S(2)}) collective-permute-start(f32[64,3072]{1,0:T(8,128)S(1)} %get-tuple-element.63), channel_id=1, source_target_pairs={{0,2},{1,3},{2,0},{3,1},{4,8},{5,9},{6,10},{7,11},{8,4},{9,5},{10,... | collective-permute-start | bytes 2359304 | tf_op jit(solution)/shard_map/ppermute | solution.py:262
  212.9 42.4 %collective-permute-start.14 = (f32[64,3072]{1,0:T(8,128)S(1)}, f32[64,3072]{1,0:T(8,128)S(1)}, u32[]{:S(2)}, u32[]{:S(2)}) collective-permute-start(f32[64,3072]{1,0:T(8,128)S(1)} %get-tuple-element.69), channel_id=1, source_target_pairs={{0,7},{1,6},{2,5},{3,4},{4,13},{5,12},{6,15},{7,14},{8,1},{9,0},{1... | collective-permute-start | bytes 2359304 | tf_op jit(solution)/shard_map/ppermute | solution.py:262
  239.5 32.9 %collective-permute-start.15 = (f32[64,3072]{1,0:T(8,128)S(1)}, f32[64,3072]{1,0:T(8,128)S(1)}, u32[]{:S(2)}, u32[]{:S(2)}) collective-permute-start(f32[64,3072]{1,0:T(8,128)S(1)} %get-tuple-element.70), channel_id=1, source_target_pairs={{0,5},{1,4},{2,7},{3,6},{4,15},{5,14},{6,13},{7,12},{8,3},{9,2},{1... | collective-permute-start | bytes 2359304 | tf_op jit(solution)/shard_map/ppermute | solution.py:262
  239.5 35.4 %collective-permute-start.9 = (f32[64,3072]{1,0:T(8,128)S(1)}, f32[64,3072]{1,0:T(8,128)S(1)}, u32[]{:S(2)}, u32[]{:S(2)}) collective-permute-start(f32[64,3072]{1,0:T(8,128)S(1)} %get-tuple-element.64), channel_id=1, source_target_pairs={{0,4},{1,5},{2,6},{3,7},{4,14},{5,15},{6,12},{7,13},{8,2},{9,3},{1... | collective-permute-start | bytes 2359304 | tf_op jit(solution)/shard_map/ppermute | solution.py:262
  239.5 35.4 %collective-permute-start.10 = (f32[64,3072]{1,0:T(8,128)S(1)}, f32[64,3072]{1,0:T(8,128)S(1)}, u32[]{:S(2)}, u32[]{:S(2)}) collective-permute-start(f32[64,3072]{1,0:T(8,128)S(1)} %get-tuple-element.65), channel_id=1, source_target_pairs={{0,6},{1,7},{2,4},{3,5},{4,12},{5,13},{6,14},{7,15},{8,0},{9,1},{1... | collective-permute-start | bytes 2359304 | tf_op jit(solution)/shard_map/ppermute | solution.py:262

commit v6 on v5

--- a/solution.py
+++ b/solution.py
@@ -280,12 +280,12 @@
     factors = factor_first, factor_second
 
     pieces, names = [], []
-    for flip in range(HALVES):
-        for some in (order[:2], order[2:]):
+    for some in (order[:2], order[2:]):
+        for flip in range(HALVES):
             for j, piece in zip(some, update(where, zt, total, factors, high, low, flip, some, places)):
                 pieces.append(permute(piece, lambda c, h, p: (h, c ^ flip, partner(p, j, c, h))))
                 names.append((flip, j))
-    last = (3, 6, 7)
+    last = (5, 6, 7)
     out = None
     for some in ([i for i in range(len(pieces)) if i not in last], last):
         out = gather(where, [pieces[i] for i in some], [names[i] for i in some], places, out)

time: 277 us -> 269 us (0.971)
  waiting for transfers between devices: 91.4 us -> 66.9 us
  starting transfers between devices: 16.9 us -> 34.2 us
    ppermute x12, waiting for transfers between devices: 88.5 us -> 65.7 us  [permute(): lax.ppermute(piece, INNER, [(i, index.index(target(*at))) for i, at in en...]
    ppermute x4, starting transfers between devices: 0.6 us -> 15.9 us  [body(): other = [lax.ppermute(piece, 'core', [(0, 1), (1, 0)]) for piece in own]]
where the time goes in v6:
time: 269 us
  blocking collectives  135 us (50%)
  waiting for transfers between devices  66.9 us (25%)
  starting transfers between devices  34.2 us (13%)
  Pallas kernels  29.3 us (11%)
  local copies, waits for them, and re-layouts  3.56 us (1%)
    all_to_all x1, blocking collectives, body(): zt = lax.all_to_all(zt, CHIPS, split_axis=0, concat_axis=0, tiled=True)  83.9 us
    ppermute x12, waiting for transfers between devices, permute(): lax.ppermute(piece, INNER, [(i, index.index(target(*at))) for i, at in en...  65.7 us
    all_to_all x1, blocking collectives, body(): lax.all_to_all(partial, CHIPS, split_axis=0, concat_axis=0, tiled=True)  26.1 us
    all_to_all x1, blocking collectives, body(): lax.all_to_all(add_up(parts), CHIPS, split_axis=0, concat_axis=0, tiled=T...  24.5 us
    ppermute x12, starting transfers between devices, permute(): lax.ppermute(piece, INNER, [(i, index.index(target(*at))) for i, at in en...  18.2 us
    ppermute x4, starting transfers between devices, body(): other = [lax.ppermute(piece, 'core', [(0, 1), (1, 0)]) for piece in own]  15.9 us
    pallas_call x4, Pallas kernels, update(): pl.pallas_call(kernel, out_shape=[f32(block, rows)] * count, grid_spec=pl...  13.8 us
  transfers between devices with their start and end apart: 16, of which 8 were waited for; matrix products, arithmetic and copies ran while one was open for 0% of the time, Pallas kernels for 5%

profile of v6, /device:TPU:0, one launch (start us, length us, event | category | flops | bytes accessed | tf_op | source)
XLA Modules:
  0.0 268.8 jit_solution(5455025554511035875)
XLA Ops:
  4.3 4.0 %collective-permute-start.3 = (f32[64,3072]{1,0:T(8,128)S(1)}, f32[64,3072]{1,0:T(8,128)S(1)}, u32[]{:S(2)}, u32[]{:S(2)}) collective-permute-start(f32[64,3072]{1,0:T(8,128)S(1)} %get-tuple-element.41), channel_id=1, source_target_pairs={{0,2},{1,3},{2,0},{3,1},{4,8},{5,9},{6,10},{7,11},{8,4},{9,5},{10,... | collective-permute-start | bytes 2359304 | tf_op jit(solution)/shard_map/ppermute | solution.py:262
  10.2 10.2 %collective-permute-start.6 = (f32[64,3072]{1,0:T(8,128)S(1)}, f32[64,3072]{1,0:T(8,128)S(1)}, u32[]{:S(2)}, u32[]{:S(2)}) collective-permute-start(f32[64,3072]{1,0:T(8,128)S(1)} %collective-permute-done.2.refs_2_), channel_id=1, source_target_pairs={{0,8},{8,0},{1,9},{9,1},{2,10},{10,2},{3,11},{11,3},{4,12},{12,4},... | collective-permute-start | bytes 2359304 | tf_op jit(solution)/shard_map/ppermute | solution.py:268
  20.4 6.4 %collective-permute-done.3.refs_3_ = f32[64,3072]{1,0:T(8,128)S(1)} collective-permute-done((f32[64,3072]{1,0:T(8,128)S(1)}, f32[64,3072]{1,0:T(8,128)S(1)}, u32[]{:S(2)}, u32[]{:S(2)}) %collective-permute-start.3) | collective-permute-done | bytes 786464 | tf_op jit(solution)/shard_map/ppermute | solution.py:262
  26.8 2.1 collective-permute-start.7
  28.9 6.2 %collective-permute-done.refs_0_ = f32[64,3072]{1,0:T(8,128)S(1)} collective-permute-done((f32[64,3072]{1,0:T(8,128)S(1)}, f32[64,3072]{1,0:T(8,128)S(1)}, u32[]{:S(2)}, u32[]{:S(2)}) %collective-permute-start) | collective-permute-done | bytes 786464 | tf_op jit(solution)/shard_map/ppermute | solution.py:262
  35.1 2.5 collective-permute-start.4
  37.6 7.0 %collective-permute-done.1.refs_1_ = f32[64,3072]{1,0:T(8,128)S(1)} collective-permute-done((f32[64,3072]{1,0:T(8,128)S(1)}, f32[64,3072]{1,0:T(8,128)S(1)}, u32[]{:S(2)}, u32[]{:S(2)}) %collective-permute-start.1) | collective-permute-done | bytes 786464 | tf_op jit(solution)/shard_map/ppermute | solution.py:262
  47.7 83.9 %all_to_all.15 = f32[64,8,3072]{2,1,0:T(8,128)S(1)} all-to-all(f32[64,8,3072]{2,1,0:T(8,128)S(1)} %bitcast.33), channel_id=1, replica_groups=mesh['block'=8,'core'=2,'half'=2,'place'=4] {'half','place','block'}, dimensions={0} | all-to-all | bytes 12582912 | tf_op jit(solution)/shard_map/all_to_all | solution.py:271
  131.6 4.3 %prepare.1 = (bf16[512,3072]{1,0:T(8,128)(2,1)S(1)}, bf16[512,3072]{1,0:T(8,128)(2,1)S(1)}, f32[64,8,128]{2,1,0:T(8,128)S(1)}) custom-call(s32[3]{0:T(128)S(1)} %pad_add_fusion.where_ref, f32[64,3072]{1,0:T(8,128)S(1)} %collective-permute-done.refs_0_, f32[64,3072]{1,0:T(8,128)S(1)} %collective-permute-done.1.refs_1_, ...), custom_call_target="tpu_custom_call" | custom-call | tf_op jit(solution)/shard_map/prepare/pallas_call | solution.py:120
  135.9 5.3 %project.1 = f32[64,8,640]{2,1,0:T(8,128)S(1)} custom-call(f32[512,3072]{1,0:T(8,128)S(1)} %bitcast.12, bf16[512,3072]{1,0:T(8,128)(2,1)S(1)} %get-tuple-element.60.high_ref.refs_5_, bf16[512,3072]{1,0:T(8,128)(2,1)S(1)} %get-tuple-element.61.low_ref.refs_6_, f32[64,8,128]{2,1,0:T(8,128)S(1)} %get-tuple-element.62.overlap_ref), custom_call_target="tpu_custom_call" | custom-call | tf_op jit(solution)/shard_map/project/pallas_call | solution.py:146
  141.2 26.1 %all_to_all.16.in_ref = f32[64,8,640]{2,1,0:T(8,128)S(1)} all-to-all(f32[64,8,640]{2,1,0:T(8,128)S(1)} %project.1), channel_id=1, replica_groups=mesh['block'=8,'core'=2,'half'=2,'place'=4] {'half','place','block'}, dimensions={0} | all-to-all | bytes 2621440 | tf_op jit(solution)/shard_map/all_to_all | solution.py:277
  167.5 24.5 %all_to_all.17 = f32[64,8,640]{2,1,0:T(8,128)S(1)} all-to-all(f32[64,8,640]{2,1,0:T(8,128)S(1)} %add_up.1), channel_id=1, replica_groups=mesh['block'=8,'core'=2,'half'=2,'place'=4] {'half','place','block'}, dimensions={0} | all-to-all | bytes 2621440 | tf_op jit(solution)/shard_map/all_to_all | solution.py:278
  192.0 3.4 %update.7 = (f32[64,3072]{1,0:T(8,128)S(1)}, f32[64,3072]{1,0:T(8,128)S(1)}) custom-call(s32[3]{0:T(128)S(1)} %pad_add_fusion.where_ref, f32[8,8,8,3072]{3,2,1,0:T(8,128)S(1)} %bitcast.13, f32[8,8,8,3072]{3,2,1,0:T(8,128)S(1)} %bitcast.14, f32[8,8,8,640]{3,2,1,0:T(8,128)S(1)} %bitcast.21, f32[256,256]{1,0:T(8,128)S(1)} %copy-done.2, ...), custom_call_target="tpu_custom_call" | custom-call | tf_op jit(solution)/shard_map/update/pallas_call | solution.py:214
  196.6 3.4 %update.6 = (f32[64,3072]{1,0:T(8,128)S(1)}, f32[64,3072]{1,0:T(8,128)S(1)}) custom-call(s32[3]{0:T(128)S(1)} %pad_add_fusion.where_ref, f32[8,8,8,3072]{3,2,1,0:T(8,128)S(1)} %bitcast.15, f32[8,8,8,3072]{3,2,1,0:T(8,128)S(1)} %bitcast.16, f32[8,8,8,640]{3,2,1,0:T(8,128)S(1)} %bitcast.22, f32[256,256]{1,0:T(8,128)S(1)} %copy-done.2, ...), custom_call_target="tpu_custom_call" | custom-call | tf_op jit(solution)/shard_map/update/pallas_call | solution.py:214
  200.1 2.6 collective-permute-start.11
  202.7 3.4 %update.5 = (f32[64,3072]{1,0:T(8,128)S(1)}, f32[64,3072]{1,0:T(8,128)S(1)}) custom-call(s32[3]{0:T(128)S(1)} %pad_add_fusion.where_ref, f32[8,8,8,3072]{3,2,1,0:T(8,128)S(1)} %bitcast.17, f32[8,8,8,3072]{3,2,1,0:T(8,128)S(1)} %bitcast.18, f32[8,8,8,640]{3,2,1,0:T(8,128)S(1)} %bitcast.23, f32[256,256]{1,0:T(8,128)S(1)} %copy-done.2, ...), custom_call_target="tpu_custom_call" | custom-call | tf_op jit(solution)/shard_map/update/pallas_call | solution.py:214
  206.1 3.4 %update.4 = (f32[64,3072]{1,0:T(8,128)S(1)}, f32[64,3072]{1,0:T(8,128)S(1)}) custom-call(s32[3]{0:T(128)S(1)} %pad_add_fusion.where_ref, f32[8,8,8,3072]{3,2,1,0:T(8,128)S(1)} %bitcast.19, f32[8,8,8,3072]{3,2,1,0:T(8,128)S(1)} %bitcast.20, f32[8,8,8,640]{3,2,1,0:T(8,128)S(1)} %bitcast.24, f32[256,256]{1,0:T(8,128)S(1)} %copy-done.2, ...), custom_call_target="tpu_custom_call" | custom-call | tf_op jit(solution)/shard_map/update/pallas_call | solution.py:214
  211.5 15.0 %collective-permute-done.13.refs_2_ = f32[64,3072]{1,0:T(8,128)S(1)} collective-permute-done((f32[64,3072]{1,0:T(8,128)S(1)}, f32[64,3072]{1,0:T(8,128)S(1)}, u32[]{:S(2)}, u32[]{:S(2)}) %collective-permute-start.13) | collective-permute-done | bytes 786464 | tf_op jit(solution)/shard_map/ppermute | solution.py:262
  227.3 5.9 %collective-permute-start.10 = (f32[64,3072]{1,0:T(8,128)S(1)}, f32[64,3072]{1,0:T(8,128)S(1)}, u32[]{:S(2)}, u32[]{:S(2)}) collective-permute-start(f32[64,3072]{1,0:T(8,128)S(1)} %get-tuple-element.65), channel_id=1, source_target_pairs={{0,6},{1,7},{2,4},{3,5},{4,12},{5,13},{6,14},{7,15},{8,0},{9,1},{1... | collective-permute-start | bytes 2359304 | tf_op jit(solution)/shard_map/ppermute | solution.py:262
  233.2 22.5 %collective-permute-done.12.refs_1_ = f32[64,3072]{1,0:T(8,128)S(1)} collective-permute-done((f32[64,3072]{1,0:T(8,128)S(1)}, f32[64,3072]{1,0:T(8,128)S(1)}, u32[]{:S(2)}, u32[]{:S(2)}) %collective-permute-start.12) | collective-permute-done | bytes 786464 | tf_op jit(solution)/shard_map/ppermute | solution.py:262
  255.6 2.5 gather.2.refs_3_
  258.2 2.4 collective-permute-done.9.refs_1_
  260.5 6.2 %collective-permute-done.8.refs_0_ = f32[64,3072]{1,0:T(8,128)S(1)} collective-permute-done((f32[64,3072]{1,0:T(8,128)S(1)}, f32[64,3072]{1,0:T(8,128)S(1)}, u32[]{:S(2)}, u32[]{:S(2)}) %collective-permute-start.8) | collective-permute-done | bytes 786464 | tf_op jit(solution)/shard_map/ppermute | solution.py:262
  266.7 2.0 gather.3
  (34 shorter events, 13.1 us)
Async XLA Ops:
  0.1 1.4 copy-start
  1.5 1.4 copy-start.1
  3.5 6.6 %collective-permute-start.2 = (f32[64,3072]{1,0:T(8,128)S(1)}, f32[64,3072]{1,0:T(8,128)S(1)}, u32[]{:S(2)}, u32[]{:S(2)}) collective-permute-start(f32[64,3072]{1,0:T(8,128)S(1)} %get-tuple-element.40), channel_id=1, source_target_pairs={{0,0},{1,1},{2,2},{3,3},{4,10},{5,11},{6,8},{7,9},{8,6},{9,7},{10,... | collective-permute-start | bytes 2359304 | tf_op jit(solution)/shard_map/ppermute | solution.py:262
  4.3 41.5 %copy-start.4 = (f32[8,196608]{1,0:T(8,128)S(1)}, f32[8,196608]{1,0:T(8,128)}, u32[]{:S(2)}) copy-start(f32[8,196608]{1,0:T(8,128)} %param.5) | copy-start | bytes 18874372
  4.3 22.5 %collective-permute-start.3 = (f32[64,3072]{1,0:T(8,128)S(1)}, f32[64,3072]{1,0:T(8,128)S(1)}, u32[]{:S(2)}, u32[]{:S(2)}) collective-permute-start(f32[64,3072]{1,0:T(8,128)S(1)} %get-tuple-element.41), channel_id=1, source_target_pairs={{0,2},{1,3},{2,0},{3,1},{4,8},{5,9},{6,10},{7,11},{8,4},{9,5},{10,... | collective-permute-start | bytes 2359304 | tf_op jit(solution)/shard_map/ppermute | solution.py:262
  9.0 26.2 %collective-permute-start = (f32[64,3072]{1,0:T(8,128)S(1)}, f32[64,3072]{1,0:T(8,128)S(1)}, u32[]{:S(2)}, u32[]{:S(2)}) collective-permute-start(f32[64,3072]{1,0:T(8,128)S(1)} %get-tuple-element.38), channel_id=1, source_target_pairs={{0,3},{1,2},{2,1},{3,0},{4,9},{5,8},{6,11},{7,10},{8,5},{9,4},{10,... | collective-permute-start | bytes 2359304 | tf_op jit(solution)/shard_map/ppermute | solution.py:262
  9.8 34.9 %collective-permute-start.1 = (f32[64,3072]{1,0:T(8,128)S(1)}, f32[64,3072]{1,0:T(8,128)S(1)}, u32[]{:S(2)}, u32[]{:S(2)}) collective-permute-start(f32[64,3072]{1,0:T(8,128)S(1)} %get-tuple-element.39), channel_id=1, source_target_pairs={{0,1},{1,0},{2,3},{3,2},{4,11},{5,10},{6,9},{7,8},{8,7},{9,6},{10,... | collective-permute-start | bytes 2359304 | tf_op jit(solution)/shard_map/ppermute | solution.py:262
  10.2 36.4 %collective-permute-start.6 = (f32[64,3072]{1,0:T(8,128)S(1)}, f32[64,3072]{1,0:T(8,128)S(1)}, u32[]{:S(2)}, u32[]{:S(2)}) collective-permute-start(f32[64,3072]{1,0:T(8,128)S(1)} %collective-permute-done.2.refs_2_), channel_id=1, source_target_pairs={{0,8},{8,0},{1,9},{9,1},{2,10},{10,2},{3,11},{11,3},{4,12},{12,4},... | collective-permute-start | bytes 2359304 | tf_op jit(solution)/shard_map/ppermute | solution.py:268
  26.8 19.7 %collective-permute-start.7 = (f32[64,3072]{1,0:T(8,128)S(1)}, f32[64,3072]{1,0:T(8,128)S(1)}, u32[]{:S(2)}, u32[]{:S(2)}) collective-permute-start(f32[64,3072]{1,0:T(8,128)S(1)} %collective-permute-done.3.refs_3_), channel_id=1, source_target_pairs={{0,8},{8,0},{1,9},{9,1},{2,10},{10,2},{3,11},{11,3},{4,12},{12,4},... | collective-permute-start | bytes 2359304 | tf_op jit(solution)/shard_map/ppermute | solution.py:268
  35.1 11.4 %collective-permute-start.4 = (f32[64,3072]{1,0:T(8,128)S(1)}, f32[64,3072]{1,0:T(8,128)S(1)}, u32[]{:S(2)}, u32[]{:S(2)}) collective-permute-start(f32[64,3072]{1,0:T(8,128)S(1)} %collective-permute-done.refs_0_), channel_id=1, source_target_pairs={{0,8},{8,0},{1,9},{9,1},{2,10},{10,2},{3,11},{11,3},{4,12},{12,4},... | collective-permute-start | bytes 2359304 | tf_op jit(solution)/shard_map/ppermute | solution.py:268
  44.6 3.1 %collective-permute-start.5 = (f32[64,3072]{1,0:T(8,128)S(1)}, f32[64,3072]{1,0:T(8,128)S(1)}, u32[]{:S(2)}, u32[]{:S(2)}) collective-permute-start(f32[64,3072]{1,0:T(8,128)S(1)} %collective-permute-done.1.refs_1_), channel_id=1, source_target_pairs={{0,8},{8,0},{1,9},{9,1},{2,10},{10,2},{3,11},{11,3},{4,12},{12,4},... | collective-permute-start | bytes 2359304 | tf_op jit(solution)/shard_map/ppermute | solution.py:268
  167.3 24.7 %copy-start.2 = (f32[256,256]{1,0:T(8,128)S(1)}, f32[256,256]{1,0:T(8,128)}, u32[]{:S(2)}) copy-start(f32[256,256]{1,0:T(8,128)} %refs_3_.7) | copy-start | bytes 786436
  167.3 24.7 %copy-start.3 = (f32[256,256]{1,0:T(8,128)S(1)}, f32[256,256]{1,0:T(8,128)}, u32[]{:S(2)}) copy-start(f32[256,256]{1,0:T(8,128)} %refs_4_.7) | copy-start | bytes 786436
  195.5 31.1 %collective-permute-start.13 = (f32[64,3072]{1,0:T(8,128)S(1)}, f32[64,3072]{1,0:T(8,128)S(1)}, u32[]{:S(2)}, u32[]{:S(2)}) collective-permute-start(f32[64,3072]{1,0:T(8,128)S(1)} %get-tuple-element.68), channel_id=1, source_target_pairs={{0,7},{1,6},{2,5},{3,4},{4,13},{5,12},{6,15},{7,14},{8,1},{9,0},{1... | collective-permute-start | bytes 2359304 | tf_op jit(solution)/shard_map/ppermute | solution.py:262
  196.6 30.7 %collective-permute-start.14 = (f32[64,3072]{1,0:T(8,128)S(1)}, f32[64,3072]{1,0:T(8,128)S(1)}, u32[]{:S(2)}, u32[]{:S(2)}) collective-permute-start(f32[64,3072]{1,0:T(8,128)S(1)} %get-tuple-element.69), channel_id=1, source_target_pairs={{0,5},{1,4},{2,7},{3,6},{4,15},{5,14},{6,13},{7,12},{8,3},{9,2},{1... | collective-permute-start | bytes 2359304 | tf_op jit(solution)/shard_map/ppermute | solution.py:262
  200.1 33.1 %collective-permute-start.11 = (f32[64,3072]{1,0:T(8,128)S(1)}, f32[64,3072]{1,0:T(8,128)S(1)}, u32[]{:S(2)}, u32[]{:S(2)}) collective-permute-start(f32[64,3072]{1,0:T(8,128)S(1)} %get-tuple-element.66), channel_id=1, source_target_pairs={{0,3},{1,2},{2,1},{3,0},{4,9},{5,8},{6,11},{7,10},{8,5},{9,4},{10,... | collective-permute-start | bytes 2359304 | tf_op jit(solution)/shard_map/ppermute | solution.py:262
  209.6 46.1 %collective-permute-start.12 = (f32[64,3072]{1,0:T(8,128)S(1)}, f32[64,3072]{1,0:T(8,128)S(1)}, u32[]{:S(2)}, u32[]{:S(2)}) collective-permute-start(f32[64,3072]{1,0:T(8,128)S(1)} %get-tuple-element.67), channel_id=1, source_target_pairs={{0,1},{1,0},{2,3},{3,2},{4,11},{5,10},{6,9},{7,8},{8,7},{9,6},{10,... | collective-permute-start | bytes 2359304 | tf_op jit(solution)/shard_map/ppermute | solution.py:262
  209.7 50.9 %collective-permute-start.9 = (f32[64,3072]{1,0:T(8,128)S(1)}, f32[64,3072]{1,0:T(8,128)S(1)}, u32[]{:S(2)}, u32[]{:S(2)}) collective-permute-start(f32[64,3072]{1,0:T(8,128)S(1)} %get-tuple-element.64), channel_id=1, source_target_pairs={{0,4},{1,5},{2,6},{3,7},{4,14},{5,15},{6,12},{7,13},{8,2},{9,3},{1... | collective-permute-start | bytes 2359304 | tf_op jit(solution)/shard_map/ppermute | solution.py:262
  226.5 29.1 %collective-permute-start.15 = (f32[64,3072]{1,0:T(8,128)S(1)}, f32[64,3072]{1,0:T(8,128)S(1)}, u32[]{:S(2)}, u32[]{:S(2)}) collective-permute-start(f32[64,3072]{1,0:T(8,128)S(1)} %get-tuple-element.70), channel_id=1, source_target_pairs={{0,0},{1,1},{2,2},{3,3},{4,10},{5,11},{6,8},{7,9},{8,6},{9,7},{10,... | collective-permute-start | bytes 2359304 | tf_op jit(solution)/shard_map/ppermute | solution.py:262
  227.3 33.3 %collective-permute-start.10 = (f32[64,3072]{1,0:T(8,128)S(1)}, f32[64,3072]{1,0:T(8,128)S(1)}, u32[]{:S(2)}, u32[]{:S(2)}) collective-permute-start(f32[64,3072]{1,0:T(8,128)S(1)} %get-tuple-element.65), channel_id=1, source_target_pairs={{0,6},{1,7},{2,4},{3,5},{4,12},{5,13},{6,14},{7,15},{8,0},{9,1},{1... | collective-permute-start | bytes 2359304 | tf_op jit(solution)/shard_map/ppermute | solution.py:262
  233.2 33.6 %collective-permute-start.8 = (f32[64,3072]{1,0:T(8,128)S(1)}, f32[64,3072]{1,0:T(8,128)S(1)}, u32[]{:S(2)}, u32[]{:S(2)}) collective-permute-start(f32[64,3072]{1,0:T(8,128)S(1)} %get-tuple-element.63), channel_id=1, source_target_pairs={{0,2},{1,3},{2,0},{3,1},{4,8},{5,9},{6,10},{7,11},{8,4},{9,5},{10,... | collective-permute-start | bytes 2359304 | tf_op jit(solution)/shard_map/ppermute | solution.py:262
